TPU v7x, 256 devices: a whole 4x4x8 slice. The times are simulated.
256 devices in a mesh: frame: 8 (over y, core), space: 32 (over z, x).
Axes of the slice: x: 4, y: 4, z: 8, core: 2. Of those that a mesh axis runs over, the one named last changes fastest.
Arguments:
- latents: bfloat16 [8, 64, 64, 768], P('frame', 'space'), may hold values from -6 to 6
- occupancy: int32 [64, 64], P('space'), may hold values 0 or 1
- neighbors: int32 [64, 6], P('space'), may hold values from -1 to 63, as said below
- brick_counts: int32 [64], replicated, may hold values from 1 to 64, as said below
- noise_levels: int32 [8], P('frame'), may hold values from 0 to 15
- level_embed: float32 [16, 768], replicated, may hold values from -6 to 6
- occupied_embed: float32 [768], replicated, may hold values from -6 to 6
- step_size: float32 [16], replicated, may hold values from 0.25 to 1
- fresh_noise: bfloat16 [64, 64, 768], P('space'), may hold values from -6 to 6
- space_project: bfloat16 [768, 2304], replicated, may hold values from -2 to 2
- space_output: bfloat16 [768, 768], replicated, may hold values from -0.21875 to 0.21875
- time_project: bfloat16 [768, 2304], replicated, may hold values from -2 to 2
- time_output: bfloat16 [768, 768], replicated, may hold values from -0.21875 to 0.21875
- expand_weight: bfloat16 [768, 1536], P(None, 'space'), may hold values from -0.21875 to 0.21875
- reduce_weight: bfloat16 [1536, 768], P('space'), may hold values from -0.15625 to 0.15625
Outputs:
- generated: bfloat16 [8, 64, 64, 768], P('frame', 'space')
Inputs may be any that keep to these rules, and one draw needn't show every extreme that they name: `neighbors`: each entry is -1 (no brick there) or the index of another brick of the same frame whose index differs from the row's own by 1 to 2; a difference of exactly 2 occurs in every draw. `brick_counts`: the valid tokens of a brick are its first ones; some brick is full.
All inputs are finite; a program needn't handle non-finite values. No bound on the sum of `occupancy` on one device may be relied on, other than what follows from the above.
Results may differ from a plain program's by a relative error of at most 0.02.
Values may be sent and summed in bfloat16 or wider, within the bound.
No kernel may reach another device: no remote copies, remote signals or barrier semaphores. Data moves between devices by JAX's collectives and lax.ppermute only.
A program may use at most 128 MiB of HBM per device.

v0:
```python
import functools

import jax
import jax.numpy as jnp
from jax import lax
from jax.experimental import pallas as pl
from jax.experimental.pallas import tpu as pltpu
from jax.sharding import PartitionSpec as P

HEADS = 12
FRAMES = 8
YS = 4
EPSILON = 1e-06
MASKED = -1e30

F32 = jnp.float32
BF16 = jnp.bfloat16
VMEM_LIMIT = 24 * 1024 * 1024

I_FRAME, I_SPACE, I_Y, I_CORE, I_LEVEL = range(5)

vmem = pl.BlockSpec(memory_space=pltpu.VMEM)
smem = pl.BlockSpec(memory_space=pltpu.SMEM)
anywhere = pl.BlockSpec(memory_space=pl.ANY)


def dot(a, b):
    return jnp.dot(a, b, preferred_element_type=F32)


def dot_t(a, b):
    return lax.dot_general(a, b, (((1,), (1,)), ((), ())), preferred_element_type=F32)


def rms(values):
    return values * lax.rsqrt(jnp.mean(values * values, axis=-1, keepdims=True) + EPSILON)


def chunk_rows(index, rows):
    return pl.ds(pl.multiple_of(index * rows, rows), rows)


def call(kernel, outs, specs, scratch=(), waits=(), limit=VMEM_LIMIT):
    used = len(specs)
    specs = specs + [anywhere] * len(waits)

    def body(*refs):
        kernel(*refs[:used], *refs[used + len(waits) :])

    return functools.partial(pallas(body, outs, specs, scratch, limit), waits)


def pallas(kernel, outs, specs, scratch, limit):
    made = pl.pallas_call(
        kernel,
        out_shape=outs,
        in_specs=specs,
        out_specs=jax.tree.map(lambda _: vmem, outs),
        scratch_shapes=scratch,
        compiler_params=pltpu.CompilerParams(vmem_limit_bytes=limit),
        cost_estimate=pl.CostEstimate(flops=0, bytes_accessed=1, transcendentals=0),
    )
    return lambda waits, *operands: made(*operands, *waits)


def state_before(state, occupancy, embed, level):
    size = occupancy.shape[1]
    row = lax.broadcasted_iota(jnp.int32, (size, size), 0)
    column = lax.broadcasted_iota(jnp.int32, (size, size), 1)
    marks = []
    for b in range(occupancy.shape[0]):
        spread = jnp.where(row == column, occupancy[b : b + 1, :].astype(F32), 0.0)
        marks.append(jnp.sum(spread, axis=-1, keepdims=True))
    return state.astype(F32) + jnp.concatenate(marks, axis=0) * embed + level


def pre_kernel(info, state, occupancy, levels, embed, expand, reduce, normed, piece, *rest):
    chunks = rest[:YS]
    state_in, occupancy_in, levels_in, sems = rest[YS:]
    copies = [
        pltpu.make_async_copy(source, target, sems.at[i])
        for i, (source, target) in enumerate(
            ((state, state_in), (occupancy, occupancy_in), (levels, levels_in))
        )
    ]
    for copy in copies:
        copy.start()
    first_core = info[I_CORE] == 0

    @pl.when(first_core)
    def _():
        pltpu.make_async_copy(expand, piece, sems.at[3]).start()

    @pl.when(jnp.logical_not(first_core))
    def _():
        pltpu.make_async_copy(reduce, piece, sems.at[3]).start()

    for copy in copies:
        copy.wait()
    level = levels_in[pl.ds(info[I_LEVEL], 1), :]
    before = state_before(state_in[...], occupancy_in, embed[...], level)
    normed[...] = rms(before).astype(BF16)
    send_chunks(info, normed, chunks)
    pltpu.make_async_copy(reduce, piece, sems.at[3]).wait()


def send_chunks(info, rows, chunks):
    size = rows.shape[0] // YS
    for k, chunk in enumerate(chunks):
        chunk[...] = rows[chunk_rows(lax.rem(info[I_Y] + k, YS), size), :]


def time_project_kernel(shift, info, c0, c1, c2, c3, project, queries, pairs, rows):
    size = c0.shape[0]
    for k, chunk in enumerate((c0, c1, c2, c3)):
        at = lax.rem(info[I_Y] + YS - k + shift * (YS - info[I_CORE]), YS)
        rows[chunk_rows(at, size), :] = chunk[...]
    width = rows.shape[1]
    values = rows[...]
    pairs[...] = dot(values, project[:, width:]).astype(BF16)
    queries[...] = dot(values, project[:, :width]).astype(BF16)


def head_selector(width):
    lane = lax.broadcasted_iota(jnp.int32, (width, 128), 0)
    head = lax.broadcasted_iota(jnp.int32, (width, 128), 1)
    return (lane // (width // HEADS) == head).astype(BF16)


def head_spreader(width):
    head = lax.broadcasted_iota(jnp.int32, (128, width), 0)
    lane = lax.broadcasted_iota(jnp.int32, (128, width), 1)
    return (lane // (width // HEADS) == head).astype(BF16)


def time_attend_kernel(info, queries, mine, other, m0, m1, m2, m3, mixed):
    tokens = queries.shape[0] // YS
    width = queries.shape[1]
    scale = (width // HEADS) ** -0.5
    selector = head_selector(width)
    first_core = info[I_CORE] == 0
    scores = {}
    for side, pairs in enumerate((mine, other)):
        for i in range(YS):
            left = YS - i
            keys = pairs[i * tokens : (i + 1) * tokens, :width].astype(F32)
            query = queries[i * tokens :, :].astype(F32).reshape(left, tokens, width)
            product = (query * keys[None]).reshape(left * tokens, width)
            high = product.astype(BF16)
            low = (product - high.astype(F32)).astype(BF16)
            score = (dot(high, selector) + dot(low, selector)) * scale
            for j in range(i, YS):
                part = score[(j - i) * tokens : (j - i + 1) * tokens, :]
                if side == 1 and i == j:
                    part = jnp.where(first_core, MASKED, part)
                scores[side, i, j] = part
    weights = []
    for j in range(YS):
        parts = [scores[side, i, j] for side in range(2) for i in range(j + 1)]
        highest = parts[0]
        for part in parts[1:]:
            highest = jnp.maximum(highest, part)
        raised = [jnp.exp(part - highest) for part in parts]
        total = raised[0]
        for part in raised[1:]:
            total = total + part
        weights += [(part / total).astype(BF16) for part in raised]
    spread = dot(jnp.concatenate(weights, axis=0), head_spreader(width))
    at = 0
    for j in range(YS):
        mix = None
        for pairs in (mine, other):
            for i in range(j + 1):
                value = pairs[i * tokens : (i + 1) * tokens, width:].astype(F32)
                term = spread[at * tokens : (at + 1) * tokens, :] * value
                mix = term if mix is None else mix + term
                at += 1
        mixed[j * tokens : (j + 1) * tokens, :] = mix.astype(BF16)
    send_chunks(info, mixed, (m0, m1, m2, m3))


def space_project_kernel(info, state, occupied, embed, levels, left, right, project, queries, pairs):
    width = state.shape[1]
    count = state.shape[0]
    level = levels[pl.ds(info[I_LEVEL], 1), :]
    before = state_before(state[...], occupied, embed[...], level)
    own = rms(before).astype(BF16)
    scale = (width // HEADS) ** -0.5
    queries[...] = (dot(own, project[:, :width]).astype(BF16) * scale).astype(BF16)
    pairs[count : 2 * count, :] = dot(own, project[:, width:]).astype(BF16)
    pairs[:count, :] = dot(left[...], project[:, width:]).astype(BF16)
    pairs[2 * count :, :] = dot(right[...], project[:, width:]).astype(BF16)


def space_attend_kernel(info, neighbors, counts, queries, pairs, output, term, mixed):
    rows, width = queries.shape
    blocks = neighbors.shape[0]
    brick = rows // blocks
    keys = pairs.shape[0]
    nearby = keys // brick
    total_bricks = counts.shape[0]
    column = lax.broadcasted_iota(jnp.int32, (1, keys), 1)
    key_brick = column // brick
    slot = column % brick
    times = []
    for b in range(blocks):
        row = jnp.zeros((1, keys), F32)
        for e in range(nearby):
            index = (info[I_SPACE] - 1) * blocks + e
            inside = (index >= 0) & (index < total_bricks)
            number = jnp.int32(1 if e == blocks + b else 0)
            for n in range(neighbors.shape[1]):
                number = number + jnp.where(inside & (neighbors[b, n] == index), 1, 0)
            valid = counts[jnp.clip(index, 0, total_bricks - 1)]
            row = jnp.where((key_brick == e) & (slot < valid), number.astype(F32), row)
        times.append(jnp.broadcast_to(row, (brick, keys)))
    times = jnp.concatenate(times + times, axis=0)
    usable = times > 0.0
    pair = 2 * (width // HEADS)
    half = lax.broadcasted_iota(jnp.int32, (rows, pair), 1) < pair // 2
    for h in range(HEADS // 2):
        lanes = slice(h * pair, (h + 1) * pair)
        query = queries[:, lanes]
        zero = jnp.zeros_like(query)
        both = jnp.concatenate([jnp.where(half, query, zero), jnp.where(half, zero, query)], axis=0)
        score = jnp.where(usable, dot_t(both, pairs[:, lanes]), MASKED)
        highest = jnp.max(score, axis=-1, keepdims=True)
        raised = jnp.exp(score - highest) * times
        share = (raised / jnp.sum(raised, axis=-1, keepdims=True)).astype(BF16)
        mix = dot(share, pairs[:, width + h * pair : width + (h + 1) * pair])
        mixed[:, lanes] = jnp.where(half, mix[:rows], mix[rows:]).astype(BF16)
    term[...] = dot(mixed[...], output[...])


def finish_kernel(
    hand_on, info, steps, next_level, state, occupied, embed, levels, space_term, m0, m1, m2, m3, output, *rest
):
    weights = rest[:8]
    if hand_on:
        fresh, moved, normed = rest[8:11]
        chunks = rest[11:15]
        expand, reduce, mixed, sems = rest[15:]
    else:
        moved = rest[8]
        expand, reduce, mixed, sems = rest[9:]
    parts = len(weights) // 2
    deep = weights[0].shape[0]

    def copies(swap):
        for i in range(parts):
            first, second = (weights[parts + i], weights[i]) if swap else (weights[i], weights[parts + i])
            part = pl.ds(i * deep, deep)
            pltpu.make_async_copy(first, expand.at[part, :], sems.at[i]).start()
            pltpu.make_async_copy(second, reduce.at[part, :], sems.at[parts + i]).start()

    core = info[I_CORE]

    @pl.when(core == 0)
    def _():
        copies(False)

    @pl.when(core != 0)
    def _():
        copies(True)

    size = m0.shape[0]
    for k, chunk in enumerate((m0, m1, m2, m3)):
        mixed[chunk_rows(lax.rem(info[I_Y] + YS - k, YS), size), :] = chunk[...]
    level = levels[pl.ds(info[I_LEVEL], 1), :]
    current = state[...]
    before = state_before(current, occupied, embed[...], level)
    change = space_term[...] + dot(mixed[...], output[...])
    middle = rms(before + change).astype(BF16)
    for i in range(parts):
        part = pl.ds(i * deep, deep)
        pltpu.make_async_copy(weights[i], expand.at[part, :], sems.at[i]).wait()
        pltpu.make_async_copy(weights[i], reduce.at[part, :], sems.at[parts + i]).wait()
        hidden = jax.nn.gelu(dot_t(middle, expand[part, :]), approximate=True).astype(BF16)
        change = change + dot(hidden, reduce[part, :])
    result = (current.astype(F32) + steps[info[I_LEVEL]] * change).astype(BF16)
    if not hand_on:
        moved[...] = result
        return
    result = jnp.where(info[I_FRAME] == 0, fresh[...], result)
    moved[...] = result
    level = levels[pl.ds(next_level[0], 1), :]
    normed[...] = rms(state_before(result, occupied, embed[...], level)).astype(BF16)
    send_chunks(info, normed, chunks)


def shards(
    latents,
    occupancy,
    neighbors,
    brick_counts,
    noise_levels,
    level_embed,
    occupied_embed,
    step_size,
    fresh_noise,
    space_project,
    space_output,
    time_project,
    time_output,
    expand_weight,
    reduce_weight,
):
    blocks, brick, width = latents.shape[1:]
    rows = blocks * brick
    chunk = rows // YS
    frames = lax.axis_size("frame")
    spaces = lax.axis_size("space")
    xs, zs = 4, spaces // 4
    frame = lax.axis_index("frame").astype(jnp.int32)
    space = lax.axis_index("space").astype(jnp.int32)
    core = frame % 2

    def along(block, axis, route):
        return lax.ppermute(block, axis, [(i, route(i)) for i in range(lax.axis_size(axis))])

    def both(block, route):
        pairs = []
        for f in range(frames):
            for s in range(spaces):
                to_f, to_s = route(f, s)
                pairs.append((f * spaces + s, to_f * spaces + to_s))
        return lax.ppermute(block, ("frame", "space"), pairs)

    def y_on(f, k):
        return (f // 2 + k) % YS * 2 + f % 2

    level_before = along(noise_levels, "frame", lambda f: (f + 1) % frames)
    info = jnp.stack(
        [frame, space, frame // 2, core, noise_levels[0]]
    ).astype(jnp.int32)
    occupied = occupancy
    embed = occupied_embed.reshape(1, width)

    def struct(*shape, dtype=BF16):
        return jax.ShapeDtypeStruct(shape, dtype)

    chunk_structs = [struct(chunk, width)] * YS

    def attend(state, left, right, chunks, shift, waits):
        queries, pairs = call(
            lambda *refs: time_project_kernel(shift, *refs),
            [struct(rows, width), struct(rows, 2 * width)],
            [smem] + [vmem] * 5,
            [pltpu.VMEM((rows, width), BF16)],
            waits,
        )(info, *chunks, time_project)
        other_pairs = along(pairs, "frame", lambda f: f ^ 1)
        space_queries, space_pairs = call(
            space_project_kernel,
            [struct(rows, width), struct(3 * rows, 2 * width)],
            [smem] + [vmem] * 7,
        )(info, state, occupied, embed, level_embed, left, right, space_project)
        mixed = call(
            time_attend_kernel,
            chunk_structs,
            [smem] + [vmem] * 3,
            [pltpu.VMEM((rows, width), BF16)],
            [space_queries],
        )(info, queries, pairs, other_pairs)
        mixed = [mixed[0]] + [
            along(mixed[k], "frame", lambda f, k=k: y_on(f, k)) for k in range(1, YS)
        ]
        space_term = call(
            space_attend_kernel,
            struct(rows, width, dtype=F32),
            [smem] * 3 + [vmem] * 3,
            [pltpu.VMEM((rows, width), BF16)],
        )(info, neighbors, brick_counts, space_queries, space_pairs, space_output)
        return space_term, mixed

    def finish(state, space_term, mixed, mine, other, hand_on):
        hidden = 2 * sum(block.shape[0] for block in mine) // 2
        specs = [smem, smem, smem] + [vmem] * 10 + [anywhere] * 8
        operands = [info, step_size, level_before, state, occupied, embed, level_embed, space_term, *mixed]
        operands += [time_output, *mine, *other]
        outs = struct(rows, width)
        if hand_on:
            specs.append(vmem)
            operands.append(fresh_noise.reshape(rows, width))
            outs = [outs, outs] + chunk_structs
        return call(
            lambda *refs: finish_kernel(hand_on, *refs),
            outs,
            specs,
            [
                pltpu.VMEM((hidden, width), BF16),
                pltpu.VMEM((hidden, width), BF16),
                pltpu.VMEM((rows, width), BF16),
                pltpu.SemaphoreType.DMA((8,)),
            ],
        )(*operands)

    def z_on(block, k):
        return along(block, "space", lambda s: (s // xs + k) % zs * xs + s % xs)

    def x_on(block, k):
        return along(block, "space", lambda s: s // xs * xs + (s + k) % xs)

    state = latents.reshape(rows, width)
    normed, piece, *chunks = call(
        pre_kernel,
        [struct(rows, width), struct(reduce_weight.shape[0], width)] + chunk_structs,
        [smem] + [anywhere] * 3 + [vmem] + [anywhere] * 2,
        [
            pltpu.VMEM((rows, width), BF16),
            pltpu.VMEM((blocks, brick), jnp.int32),
            pltpu.VMEM(level_embed.shape, F32),
            pltpu.SemaphoreType.DMA((4,)),
        ],
        limit=60 * 1024 * 1024,
    )(info, state, occupancy, level_embed, embed, expand_weight.T, reduce_weight)
    opposite = z_on(piece, zs // 2)
    left = along(normed, "space", lambda s: (s + 1) % spaces)
    right = along(normed, "space", lambda s: (s - 1) % spaces)
    chunks = [chunks[0]] + [
        along(chunks[k], "frame", lambda f, k=k: y_on(f, k)) for k in range(1, YS)
    ]
    piece, opposite, left, right, *chunks = lax.optimization_barrier(
        (piece, opposite, left, right, *chunks)
    )
    column = jnp.concatenate([piece, opposite], axis=0)
    column = jnp.concatenate([column] + [z_on(column, k) for k in (1, 2, zs - 1)], axis=0)
    mine = [column] + [x_on(column, k) for k in (1, 3, 2)]
    space_term, mixed = attend(state, left, right, chunks, 0, [left, right])
    other = [along(mine[0], "frame", lambda f: f ^ 1)]
    space_term, *held = lax.optimization_barrier((space_term, *mixed, *mine[1:]))
    mixed, arrived = held[:YS], held[YS:]
    mine = [mine[0]] + arrived
    other += [along(block, "frame", lambda f: f ^ 1) for block in arrived]
    moved, normed, *chunks = finish(state, space_term, mixed, mine, other, True)

    chunks = [along(chunks[k], "frame", lambda f, k=k: y_on(f ^ 1, k)) for k in range(YS)]
    state = along(moved, "frame", lambda f: (f - 1) % frames)
    left = both(normed, lambda f, s: ((f - 1) % frames, (s + 1) % spaces))
    right = both(normed, lambda f, s: ((f - 1) % frames, (s - 1) % spaces))
    space_term, mixed = attend(state, left, right, chunks, 1, [state, left, right])
    return finish(state, space_term, mixed, mine, other, False).reshape(1, blocks, brick, width)


def solution(mesh):
    placed = (
        P("frame", "space", None, None),
        P("space", None),
        P("space", None),
        P(),
        P("frame"),
        P(),
        P(),
        P(),
        P("space", None, None),
        P(),
        P(),
        P(),
        P(),
        P(None, "space"),
        P("space", None),
    )
    return jax.shard_map(
        shards,
        mesh=mesh,
        in_specs=placed,
        out_specs=P("frame", "space", None, None),
        check_vma=False,
    )
```

profile of v0, /device:TPU:1, one launch (start us, length us, event | category | flops | bytes accessed | tf_op | source)
XLA Modules:
  0.0 107.9 jit_solution(10078147798998969147)
XLA Ops:
  2.6 2.8 %shard_map.145 = (bf16[128,768]{1,0:T(8,128)(2,1)}, bf16[48,768]{1,0:T(8,128)(2,1)}, bf16[32,768]{1,0:T(8,128)(2,1)}, bf16[32,768]{1,0:T(8,128)(2,1)}, bf16[32,768]{1,0:T(8,128)(2,1)}, /*index=5*/bf16[32,768]{1,0:T(8,128)(2,1)}) custom-call(s32[5]{0:T(128)} %stack.19.refs_0_, bf16[128,768]{1,0:T(8,128)(2,1)} %bitcast.8, s32[2,64]{1,0:T(2,128)} %refs_4_.7, ...), custom_call_target="tpu_custom_call" | custom-call | bytes 1 | tf_op jit(solution)/shard_map/pallas_call | solution.py:63
  5.4 2.1 %collective-permute-start.2 = (bf16[128,768]{1,0:T(8,128)(2,1)}, bf16[128,768]{1,0:T(8,128)(2,1)S(1)}, u32[]{:S(2)}, u32[]{:S(2)}) collective-permute-start(bf16[128,768]{1,0:T(8,128)(2,1)} %get-tuple-element.50), channel_id=1, source_target_pairs={{0,1},{1,2},{2,3},{3,4},{4,5},{5,6},{6,7},{7,8},{8,9},{9,10},{10,1... | collective-permute-start | bytes 589832 | tf_op jit(solution)/shard_map/ppermute | solution.py:319
  7.5 6.6 %collective-permute-start.3 = (bf16[128,768]{1,0:T(8,128)(2,1)}, bf16[128,768]{1,0:T(8,128)(2,1)S(1)}, u32[]{:S(2)}, u32[]{:S(2)}) collective-permute-start(bf16[128,768]{1,0:T(8,128)(2,1)} %get-tuple-element.50), channel_id=1, source_target_pairs={{0,31},{1,0},{2,1},{3,2},{4,3},{5,4},{6,5},{7,6},{8,7},{9,8},{10,9... | collective-permute-start | bytes 589832 | tf_op jit(solution)/shard_map/ppermute | solution.py:319
  15.4 3.8 %collective-permute-start.1 = (bf16[48,768]{1,0:T(8,128)(2,1)}, bf16[48,768]{1,0:T(8,128)(2,1)S(1)}, u32[]{:S(2)}, u32[]{:S(2)}) collective-permute-start(bf16[48,768]{1,0:T(8,128)(2,1)} %get-tuple-element.69), channel_id=1, source_target_pairs={{0,16},{1,17},{2,18},{3,19},{4,20},{5,21},{6,22},{7,23},{8,24},{9,... | collective-permute-start | bytes 221192 | tf_op jit(solution)/shard_map/ppermute | solution.py:319
  19.3 2.6 %collective-permute-start.5 = (bf16[32,768]{1,0:T(8,128)(2,1)}, bf16[32,768]{1,0:T(8,128)(2,1)S(1)}, u32[]{:S(2)}, u32[]{:S(2)}) collective-permute-start(bf16[32,768]{1,0:T(8,128)(2,1)} %get-tuple-element.53), channel_id=1, source_target_pairs={{0,128},{32,160},{64,192},{96,224},{128,0},{160,32},{192,64},{224,... | collective-permute-start | bytes 147464 | tf_op jit(solution)/shard_map/ppermute | solution.py:319
  27.5 2.0 %collective-permute-start.13 = (bf16[96,768]{1,0:T(8,128)(2,1)S(1)}, bf16[96,768]{1,0:T(8,128)(2,1)S(1)}, u32[]{:S(2)}, u32[]{:S(2)}) collective-permute-start(bf16[96,768]{1,0:T(8,128)(2,1)S(1)} %get-tuple-element.93), channel_id=1, source_target_pairs={{0,28},{1,29},{2,30},{3,31},{4,0},{5,1},{6,2},{7,3},{8,4},{9,5},{1... | collective-permute-start | bytes 442376 | tf_op jit(solution)/shard_map/ppermute | solution.py:319
  29.4 3.1 %collective-permute-done.11 = bf16[96,768]{1,0:T(8,128)(2,1)S(1)} collective-permute-done((bf16[96,768]{1,0:T(8,128)(2,1)S(1)}, bf16[96,768]{1,0:T(8,128)(2,1)S(1)}, u32[]{:S(2)}, u32[]{:S(2)}) %collective-permute-start.11) | collective-permute-done | bytes 147488 | tf_op jit(solution)/shard_map/ppermute | solution.py:319
  35.3 2.0 %collective-permute-start.15 = (bf16[384,768]{1,0:T(8,128)(2,1)S(1)}, bf16[384,768]{1,0:T(8,128)(2,1)S(1)}, u32[]{:S(2)}, u32[]{:S(2)}) collective-permute-start(bf16[384,768]{1,0:T(8,128)(2,1)S(1)} %constant_dynamic-update-slice_fusion.2.refs_13_), channel_id=1, source_target_pairs={{0,3},{1,0},{2,1},{3,2},{4,7},{5,4},{6,5},{7,6},{8,11},{9,8},{10,9... | collective-permute-start | bytes 1769480 | tf_op jit(solution)/shard_map/ppermute | solution.py:319
  38.3 2.0 %copy-done.1 = bf16[768,2304]{1,0:T(8,128)(2,1)S(1)} copy-done((bf16[768,2304]{1,0:T(8,128)(2,1)S(1)}, bf16[768,2304]{1,0:T(8,128)(2,1)}, u32[]{:S(2)}) %copy-start.1) | copy-done | bytes 3538968
  41.5 4.4 %collective-permute-start.7 = (bf16[128,1536]{1,0:T(8,128)(2,1)S(1)}, bf16[128,1536]{1,0:T(8,128)(2,1)S(1)}, u32[]{:S(2)}, u32[]{:S(2)}) collective-permute-start(bf16[128,1536]{1,0:T(8,128)(2,1)S(1)} %get-tuple-element.64.refs_2_), channel_id=1, source_target_pairs={{0,32},{32,0},{64,96},{96,64},{128,160},{160,128},{192,224},{224,1... | collective-permute-start | bytes 1179656 | tf_op jit(solution)/shard_map/ppermute | solution.py:319
  45.9 2.1 %shard_map.146 = (bf16[128,768]{1,0:T(8,128)(2,1)S(1)}, bf16[384,1536]{1,0:T(8,128)(2,1)S(1)}) custom-call(s32[5]{0:T(128)S(1)} %copy-done.9, bf16[128,768]{1,0:T(8,128)(2,1)S(1)} %bitcast.9, s32[2,64]{1,0:T(2,128)S(1)} %copy-done.11, f32[1,768]{1,0:T(1,128)S(1)} %copy-done.8, f32[16,768]{1,0:T(8,128)S(1)} %copy-done.6, ...), custom_call_target="tpu_custom_call" | custom-call | bytes 1 | tf_op jit(solution)/shard_map/pallas_call | solution.py:63
  49.9 3.4 %collective-permute-start.9 = (bf16[32,768]{1,0:T(8,128)(2,1)S(1)}, bf16[32,768]{1,0:T(8,128)(2,1)S(1)}, u32[]{:S(2)}, u32[]{:S(2)}) collective-permute-start(bf16[32,768]{1,0:T(8,128)(2,1)S(1)} %get-tuple-element.67), channel_id=1, source_target_pairs={{0,128},{32,160},{64,192},{96,224},{128,0},{160,32},{192,64},{224,... | collective-permute-start | bytes 147464 | tf_op jit(solution)/shard_map/ppermute | solution.py:319
  55.5 3.5 %shard_map.147.refs_7_ = f32[128,768]{1,0:T(8,128)S(1)} custom-call(s32[5]{0:T(128)S(1)} %copy-done.9, s32[2,6]{1,0:T(2,128)S(1)} %copy-done.12, s32[64]{0:T(128)S(1)} %copy-done.13, bf16[128,768]{1,0:T(8,128)(2,1)S(1)} %get-tuple-element.57.refs_3_.refs_4_, bf16[384,1536]{1,0:T(8,128)(2,1)S(1)} %get-tuple-element.58.refs_4_, bf16[768,768]{1,0:T(8,128)(2,1)S(1)} %copy-done.3), custom_call_target="tpu_custom_call" | custom-call | bytes 1 | tf_op jit(solution)/shard_map/pallas_call | solution.py:63
  60.6 3.6 %collective-permute-start.18 = (bf16[384,768]{1,0:T(8,128)(2,1)S(1)}, bf16[384,768]{1,0:T(8,128)(2,1)S(1)}, u32[]{:S(2)}, u32[]{:S(2)}) collective-permute-start(bf16[384,768]{1,0:T(8,128)(2,1)S(1)} %collective-permute-done.14.refs_14_), channel_id=1, source_target_pairs={{0,32},{32,0},{64,96},{96,64},{128,160},{160,128},{192,224},{224,1... | collective-permute-start | bytes 1769480 | tf_op jit(solution)/shard_map/ppermute | solution.py:319
  64.7 1.9 %collective-permute-done.refs_2_ = s32[1]{0:T(128)} collective-permute-done((s32[1]{0:T(128)}, s32[1]{0:T(128)}, u32[]{:S(2)}, u32[]{:S(2)}) %collective-permute-start) | collective-permute-done | bytes 36 | tf_op jit(solution)/shard_map/ppermute | solution.py:319
  67.5 5.3 %shard_map.150 = (bf16[128,768]{1,0:T(8,128)(2,1)S(1)}, bf16[128,768]{1,0:T(8,128)(2,1)S(1)}, bf16[32,768]{1,0:T(8,128)(2,1)S(1)}, bf16[32,768]{1,0:T(8,128)(2,1...) custom-call(s32[5]{0:T(128)S(1)} %copy-done.9, f32[16]{0:T(128)S(1)} %copy-done.14, ...), custom_call_target="tpu_custom_call" | custom-call | bytes 1 | tf_op jit(solution)/shard_map/pallas_call | solution.py:63
  72.8 2.4 %collective-permute-start.21 = (bf16[128,768]{1,0:T(8,128)(2,1)S(1)}, bf16[128,768]{1,0:T(8,128)(2,1)S(1)}, u32[]{:S(2)}, u32[]{:S(2)}) collective-permute-start(bf16[128,768]{1,0:T(8,128)(2,1)S(1)} %get-tuple-element.79), channel_id=1, source_target_pairs={{0,224},{32,0},{64,32},{96,64},{128,96},{160,128},{192,160},{224,1... | collective-permute-start | bytes 589832 | tf_op jit(solution)/shard_map/ppermute | solution.py:319
  75.2 1.9 %collective-permute-start.22 = (bf16[128,768]{1,0:T(8,128)(2,1)S(1)}, bf16[128,768]{1,0:T(8,128)(2,1)S(1)}, u32[]{:S(2)}, u32[]{:S(2)}) collective-permute-start(bf16[128,768]{1,0:T(8,128)(2,1)S(1)} %get-tuple-element.80), channel_id=1, source_target_pairs={{0,225},{1,226},{2,227},{3,228},{4,229},{5,230},{6,231},{7,232},{8... | collective-permute-start | bytes 589832 | tf_op jit(solution)/shard_map/ppermute | solution.py:327
  77.1 4.3 %collective-permute-start.23 = (bf16[128,768]{1,0:T(8,128)(2,1)S(1)}, bf16[128,768]{1,0:T(8,128)(2,1)S(1)}, u32[]{:S(2)}, u32[]{:S(2)}) collective-permute-start(bf16[128,768]{1,0:T(8,128)(2,1)S(1)} %get-tuple-element.80), channel_id=1, source_target_pairs={{0,255},{1,224},{2,225},{3,226},{4,227},{5,228},{6,229},{7,230},{8... | collective-permute-start | bytes 589832 | tf_op jit(solution)/shard_map/ppermute | solution.py:327
  83.4 3.1 %collective-permute-done.25.refs_2_ = bf16[32,768]{1,0:T(8,128)(2,1)S(1)} collective-permute-done((bf16[32,768]{1,0:T(8,128)(2,1)S(1)}, bf16[32,768]{1,0:T(8,128)(2,1)S(1)}, u32[]{:S(2)}, u32[]{:S(2)}) %collective-permute-start.25) | collective-permute-done | bytes 49184 | tf_op jit(solution)/shard_map/ppermute | solution.py:319
  88.2 2.0 %collective-permute-done.27.refs_4_ = bf16[32,768]{1,0:T(8,128)(2,1)S(1)} collective-permute-done((bf16[32,768]{1,0:T(8,128)(2,1)S(1)}, bf16[32,768]{1,0:T(8,128)(2,1)S(1)}, u32[]{:S(2)}, u32[]{:S(2)}) %collective-permute-start.27) | collective-permute-done | bytes 49184 | tf_op jit(solution)/shard_map/ppermute | solution.py:319
  91.9 2.0 %shard_map.151 = (bf16[128,768]{1,0:T(8,128)(2,1)S(1)}, bf16[384,1536]{1,0:T(8,128)(2,1)S(1)}) custom-call(s32[5]{0:T(128)S(1)} %copy-done.9, bf16[128,768]{1,0:T(8,128)(2,1)S(1)} %collective-permute-done.21.refs_1_.refs_6_.refs_3_, s32[2,64]{1,0:T(2,128)S(1)} %copy-done.11, f32[1,768]{1,0:T(1,128)S(1)} %copy-done.8, f32[16,768]{1,0:T(8,128)S(1)} %copy-done.6, ...), custom_call_target="tpu_custom_call" | custom-call | bytes 1 | tf_op jit(solution)/shard_map/pallas_call | solution.py:63
  98.5 3.5 %shard_map.152.refs_7_ = f32[128,768]{1,0:T(8,128)S(1)} custom-call(s32[5]{0:T(128)S(1)} %copy-done.9, s32[2,6]{1,0:T(2,128)S(1)} %copy-done.12, s32[64]{0:T(128)S(1)} %copy-done.13, bf16[128,768]{1,0:T(8,128)(2,1)S(1)} %get-tuple-element.81.refs_3_.refs_4_, bf16[384,1536]{1,0:T(8,128)(2,1)S(1)} %get-tuple-element.82.refs_4_, bf16[768,768]{1,0:T(8,128)(2,1)S(1)} %copy-done.3), custom_call_target="tpu_custom_call" | custom-call | bytes 1 | tf_op jit(solution)/shard_map/pallas_call | solution.py:63
  102.0 5.6 %shard_map.155 = bf16[128,768]{1,0:T(8,128)(2,1)} custom-call(s32[5]{0:T(128)S(1)} %copy-done.9, f32[16]{0:T(128)S(1)} %copy-done.14, s32[1]{0:T(128)} %collective-permute-done.refs_2_, bf16[128,768]{1,0:T(8,128)(2,1)S(1)} %collective-permute-done.21.refs_1_.refs_6_.refs_3_, s32[2,64]{1,0:T(2,128)S(1)} %copy-done.11, f32[1,768]{1,0:T(1,128)S(1)} %copy-done.8, ...), custom_call_target="tpu_custom_call" | custom-call | bytes 1 | tf_op jit(solution)/shard_map/pallas_call | solution.py:63
  (88 shorter events, 30.7 us)
Async XLA Ops:
  5.4 20.4 %collective-permute-start.2 = (bf16[128,768]{1,0:T(8,128)(2,1)}, bf16[128,768]{1,0:T(8,128)(2,1)S(1)}, u32[]{:S(2)}, u32[]{:S(2)}) collective-permute-start(bf16[128,768]{1,0:T(8,128)(2,1)} %get-tuple-element.50), channel_id=1, source_target_pairs={{0,1},{1,2},{2,3},{3,4},{4,5},{5,6},{6,7},{7,8},{8,9},{9,10},{10,1... | collective-permute-start | bytes 589832 | tf_op jit(solution)/shard_map/ppermute | solution.py:319
  7.5 18.3 %collective-permute-start.3 = (bf16[128,768]{1,0:T(8,128)(2,1)}, bf16[128,768]{1,0:T(8,128)(2,1)S(1)}, u32[]{:S(2)}, u32[]{:S(2)}) collective-permute-start(bf16[128,768]{1,0:T(8,128)(2,1)} %get-tuple-element.50), channel_id=1, source_target_pairs={{0,31},{1,0},{2,1},{3,2},{4,3},{5,4},{6,5},{7,6},{8,7},{9,8},{10,9... | collective-permute-start | bytes 589832 | tf_op jit(solution)/shard_map/ppermute | solution.py:319
  14.1 7.8 %collective-permute-start.4 = (bf16[32,768]{1,0:T(8,128)(2,1)}, bf16[32,768]{1,0:T(8,128)(2,1)S(1)}, u32[]{:S(2)}, u32[]{:S(2)}) collective-permute-start(bf16[32,768]{1,0:T(8,128)(2,1)} %get-tuple-element.52), channel_id=1, source_target_pairs={{0,64},{32,96},{64,128},{96,160},{128,192},{160,224},{192,0},{224,... | collective-permute-start | bytes 147464 | tf_op jit(solution)/shard_map/ppermute | solution.py:319
  15.4 10.3 %collective-permute-start.1 = (bf16[48,768]{1,0:T(8,128)(2,1)}, bf16[48,768]{1,0:T(8,128)(2,1)S(1)}, u32[]{:S(2)}, u32[]{:S(2)}) collective-permute-start(bf16[48,768]{1,0:T(8,128)(2,1)} %get-tuple-element.69), channel_id=1, source_target_pairs={{0,16},{1,17},{2,18},{3,19},{4,20},{5,21},{6,22},{7,23},{8,24},{9,... | collective-permute-start | bytes 221192 | tf_op jit(solution)/shard_map/ppermute | solution.py:319
  19.3 5.0 %collective-permute-start.5 = (bf16[32,768]{1,0:T(8,128)(2,1)}, bf16[32,768]{1,0:T(8,128)(2,1)S(1)}, u32[]{:S(2)}, u32[]{:S(2)}) collective-permute-start(bf16[32,768]{1,0:T(8,128)(2,1)} %get-tuple-element.53), channel_id=1, source_target_pairs={{0,128},{32,160},{64,192},{96,224},{128,0},{160,32},{192,64},{224,... | collective-permute-start | bytes 147464 | tf_op jit(solution)/shard_map/ppermute | solution.py:319
  26.7 5.9 %collective-permute-start.11 = (bf16[96,768]{1,0:T(8,128)(2,1)S(1)}, bf16[96,768]{1,0:T(8,128)(2,1)S(1)}, u32[]{:S(2)}, u32[]{:S(2)}) collective-permute-start(bf16[96,768]{1,0:T(8,128)(2,1)S(1)} %get-tuple-element.93), channel_id=1, source_target_pairs={{0,4},{1,5},{2,6},{3,7},{4,8},{5,9},{6,10},{7,11},{8,12},{9,13},{1... | collective-permute-start | bytes 442376 | tf_op jit(solution)/shard_map/ppermute | solution.py:319
  26.8 7.6 %collective-permute-start.12 = (bf16[96,768]{1,0:T(8,128)(2,1)S(1)}, bf16[96,768]{1,0:T(8,128)(2,1)S(1)}, u32[]{:S(2)}, u32[]{:S(2)}) collective-permute-start(bf16[96,768]{1,0:T(8,128)(2,1)S(1)} %get-tuple-element.93), channel_id=1, source_target_pairs={{0,8},{1,9},{2,10},{3,11},{4,12},{5,13},{6,14},{7,15},{8,16},{9,17... | collective-permute-start | bytes 442376 | tf_op jit(solution)/shard_map/ppermute | solution.py:319
  27.5 6.9 %collective-permute-start.13 = (bf16[96,768]{1,0:T(8,128)(2,1)S(1)}, bf16[96,768]{1,0:T(8,128)(2,1)S(1)}, u32[]{:S(2)}, u32[]{:S(2)}) collective-permute-start(bf16[96,768]{1,0:T(8,128)(2,1)S(1)} %get-tuple-element.93), channel_id=1, source_target_pairs={{0,28},{1,29},{2,30},{3,31},{4,0},{5,1},{6,2},{7,3},{8,4},{9,5},{1... | collective-permute-start | bytes 442376 | tf_op jit(solution)/shard_map/ppermute | solution.py:319
  34.5 26.1 %collective-permute-start.14 = (bf16[384,768]{1,0:T(8,128)(2,1)S(1)}, bf16[384,768]{1,0:T(8,128)(2,1)S(1)}, u32[]{:S(2)}, u32[]{:S(2)}) collective-permute-start(bf16[384,768]{1,0:T(8,128)(2,1)S(1)} %constant_dynamic-update-slice_fusion.2.refs_13_), channel_id=1, source_target_pairs={{0,1},{1,2},{2,3},{3,0},{4,5},{5,6},{6,7},{7,4},{8,9},{9,10},{10,1... | collective-permute-start | bytes 1769480 | tf_op jit(solution)/shard_map/ppermute | solution.py:319
  35.3 25.3 %collective-permute-start.15 = (bf16[384,768]{1,0:T(8,128)(2,1)S(1)}, bf16[384,768]{1,0:T(8,128)(2,1)S(1)}, u32[]{:S(2)}, u32[]{:S(2)}) collective-permute-start(bf16[384,768]{1,0:T(8,128)(2,1)S(1)} %constant_dynamic-update-slice_fusion.2.refs_13_), channel_id=1, source_target_pairs={{0,3},{1,0},{2,1},{3,2},{4,7},{5,4},{6,5},{7,6},{8,11},{9,8},{10,9... | collective-permute-start | bytes 1769480 | tf_op jit(solution)/shard_map/ppermute | solution.py:319
  37.3 23.3 %collective-permute-start.16 = (bf16[384,768]{1,0:T(8,128)(2,1)S(1)}, bf16[384,768]{1,0:T(8,128)(2,1)S(1)}, u32[]{:S(2)}, u32[]{:S(2)}) collective-permute-start(bf16[384,768]{1,0:T(8,128)(2,1)S(1)} %constant_dynamic-update-slice_fusion.2.refs_13_), channel_id=1, source_target_pairs={{0,2},{1,3},{2,0},{3,1},{4,6},{5,7},{6,4},{7,5},{8,10},{9,11},{10,... | collective-permute-start | bytes 1769480 | tf_op jit(solution)/shard_map/ppermute | solution.py:319
  41.5 6.5 %collective-permute-start.7 = (bf16[128,1536]{1,0:T(8,128)(2,1)S(1)}, bf16[128,1536]{1,0:T(8,128)(2,1)S(1)}, u32[]{:S(2)}, u32[]{:S(2)}) collective-permute-start(bf16[128,1536]{1,0:T(8,128)(2,1)S(1)} %get-tuple-element.64.refs_2_), channel_id=1, source_target_pairs={{0,32},{32,0},{64,96},{96,64},{128,160},{160,128},{192,224},{224,1... | collective-permute-start | bytes 1179656 | tf_op jit(solution)/shard_map/ppermute | solution.py:319
  49.8 4.6 %collective-permute-start.8 = (bf16[32,768]{1,0:T(8,128)(2,1)S(1)}, bf16[32,768]{1,0:T(8,128)(2,1)S(1)}, u32[]{:S(2)}, u32[]{:S(2)}) collective-permute-start(bf16[32,768]{1,0:T(8,128)(2,1)S(1)} %get-tuple-element.66), channel_id=1, source_target_pairs={{0,64},{32,96},{64,128},{96,160},{128,192},{160,224},{192,0},{224,... | collective-permute-start | bytes 147464 | tf_op jit(solution)/shard_map/ppermute | solution.py:319
  49.9 9.1 %collective-permute-start.9 = (bf16[32,768]{1,0:T(8,128)(2,1)S(1)}, bf16[32,768]{1,0:T(8,128)(2,1)S(1)}, u32[]{:S(2)}, u32[]{:S(2)}) collective-permute-start(bf16[32,768]{1,0:T(8,128)(2,1)S(1)} %get-tuple-element.67), channel_id=1, source_target_pairs={{0,128},{32,160},{64,192},{96,224},{128,0},{160,32},{192,64},{224,... | collective-permute-start | bytes 147464 | tf_op jit(solution)/shard_map/ppermute | solution.py:319
  54.4 6.2 %collective-permute-start.10 = (bf16[32,768]{1,0:T(8,128)(2,1)S(1)}, bf16[32,768]{1,0:T(8,128)(2,1)S(1)}, u32[]{:S(2)}, u32[]{:S(2)}) collective-permute-start(bf16[32,768]{1,0:T(8,128)(2,1)S(1)} %get-tuple-element.68), channel_id=1, source_target_pairs={{0,192},{32,224},{64,0},{96,32},{128,64},{160,96},{192,128},{224,1... | collective-permute-start | bytes 147464 | tf_op jit(solution)/shard_map/ppermute | solution.py:319
  59.0 7.6 %collective-permute-start.17 = (bf16[384,768]{1,0:T(8,128)(2,1)S(1)}, bf16[384,768]{1,0:T(8,128)(2,1)S(1)}, u32[]{:S(2)}, u32[]{:S(2)}) collective-permute-start(bf16[384,768]{1,0:T(8,128)(2,1)S(1)} %constant_dynamic-update-slice_fusion.2.refs_13_), channel_id=1, source_target_pairs={{0,32},{32,0},{64,96},{96,64},{128,160},{160,128},{192,224},{224,1... | collective-permute-start | bytes 1769480 | tf_op jit(solution)/shard_map/ppermute | solution.py:319
  60.6 6.0 %collective-permute-start.18 = (bf16[384,768]{1,0:T(8,128)(2,1)S(1)}, bf16[384,768]{1,0:T(8,128)(2,1)S(1)}, u32[]{:S(2)}, u32[]{:S(2)}) collective-permute-start(bf16[384,768]{1,0:T(8,128)(2,1)S(1)} %collective-permute-done.14.refs_14_), channel_id=1, source_target_pairs={{0,32},{32,0},{64,96},{96,64},{128,160},{160,128},{192,224},{224,1... | collective-permute-start | bytes 1769480 | tf_op jit(solution)/shard_map/ppermute | solution.py:319
  72.8 17.4 %collective-permute-start.21 = (bf16[128,768]{1,0:T(8,128)(2,1)S(1)}, bf16[128,768]{1,0:T(8,128)(2,1)S(1)}, u32[]{:S(2)}, u32[]{:S(2)}) collective-permute-start(bf16[128,768]{1,0:T(8,128)(2,1)S(1)} %get-tuple-element.79), channel_id=1, source_target_pairs={{0,224},{32,0},{64,32},{96,64},{128,96},{160,128},{192,160},{224,1... | collective-permute-start | bytes 589832 | tf_op jit(solution)/shard_map/ppermute | solution.py:319
  75.2 15.1 %collective-permute-start.22 = (bf16[128,768]{1,0:T(8,128)(2,1)S(1)}, bf16[128,768]{1,0:T(8,128)(2,1)S(1)}, u32[]{:S(2)}, u32[]{:S(2)}) collective-permute-start(bf16[128,768]{1,0:T(8,128)(2,1)S(1)} %get-tuple-element.80), channel_id=1, source_target_pairs={{0,225},{1,226},{2,227},{3,228},{4,229},{5,230},{6,231},{7,232},{8... | collective-permute-start | bytes 589832 | tf_op jit(solution)/shard_map/ppermute | solution.py:327
  77.1 13.2 %collective-permute-start.23 = (bf16[128,768]{1,0:T(8,128)(2,1)S(1)}, bf16[128,768]{1,0:T(8,128)(2,1)S(1)}, u32[]{:S(2)}, u32[]{:S(2)}) collective-permute-start(bf16[128,768]{1,0:T(8,128)(2,1)S(1)} %get-tuple-element.80), channel_id=1, source_target_pairs={{0,255},{1,224},{2,225},{3,226},{4,227},{5,228},{6,229},{7,230},{8... | collective-permute-start | bytes 589832 | tf_op jit(solution)/shard_map/ppermute | solution.py:327
  81.5 4.9 %collective-permute-start.25 = (bf16[32,768]{1,0:T(8,128)(2,1)S(1)}, bf16[32,768]{1,0:T(8,128)(2,1)S(1)}, u32[]{:S(2)}, u32[]{:S(2)}) collective-permute-start(bf16[32,768]{1,0:T(8,128)(2,1)S(1)} %get-tuple-element.84), channel_id=1, source_target_pairs={{0,96},{32,64},{64,160},{96,128},{128,224},{160,192},{192,32},{224... | collective-permute-start | bytes 147464 | tf_op jit(solution)/shard_map/ppermute | solution.py:319
  82.7 5.5 %collective-permute-start.26 = (bf16[32,768]{1,0:T(8,128)(2,1)S(1)}, bf16[32,768]{1,0:T(8,128)(2,1)S(1)}, u32[]{:S(2)}, u32[]{:S(2)}) collective-permute-start(bf16[32,768]{1,0:T(8,128)(2,1)S(1)} %get-tuple-element.85), channel_id=1, source_target_pairs={{0,160},{32,128},{64,224},{96,192},{128,32},{160,0},{192,96},{224,... | collective-permute-start | bytes 147464 | tf_op jit(solution)/shard_map/ppermute | solution.py:319
  95.8 6.2 %collective-permute-start.29 = (bf16[32,768]{1,0:T(8,128)(2,1)S(1)}, bf16[32,768]{1,0:T(8,128)(2,1)S(1)}, u32[]{:S(2)}, u32[]{:S(2)}) collective-permute-start(bf16[32,768]{1,0:T(8,128)(2,1)S(1)} %get-tuple-element.90), channel_id=1, source_target_pairs={{0,64},{32,96},{64,128},{96,160},{128,192},{160,224},{192,0},{224,... | collective-permute-start | bytes 147464 | tf_op jit(solution)/shard_map/ppermute | solution.py:319
  95.8 6.2 %collective-permute-start.30 = (bf16[32,768]{1,0:T(8,128)(2,1)S(1)}, bf16[32,768]{1,0:T(8,128)(2,1)S(1)}, u32[]{:S(2)}, u32[]{:S(2)}) collective-permute-start(bf16[32,768]{1,0:T(8,128)(2,1)S(1)} %get-tuple-element.91), channel_id=1, source_target_pairs={{0,128},{32,160},{64,192},{96,224},{128,0},{160,32},{192,64},{224,... | collective-permute-start | bytes 147464 | tf_op jit(solution)/shard_map/ppermute | solution.py:319
  (23 other events, 232.6 us)
where the time goes:
time: 108 us
  starting transfers between devices  52.6 us (49%)
  Pallas kernels  30.6 us (28%)
  waiting for transfers between devices  18.5 us (17%)
  local copies, waits for them, and re-layouts  4.92 us (5%)
  between operations  1.18 us (1%)
    ppermute x30, starting transfers between devices, along(): lax.ppermute(block, axis, [(i, route(i)) for i in range(lax.axis_size(axi...  46.4 us
    pallas_call x11, Pallas kernels, pallas(): return lambda waits, *operands: made(*operands, *waits)  30.6 us
    ppermute x30, waiting for transfers between devices, along(): lax.ppermute(block, axis, [(i, route(i)) for i in range(lax.axis_size(axi...  18.5 us
    ppermute x2, starting transfers between devices, both(): return lax.ppermute(block, ('frame', 'space'), pairs)  6.22 us
    unnamed x33, local copies, waits for them, and re-layouts  2.99 us
  transfers between devices with their start and end apart: 32, of which 11 were waited for; matrix products, arithmetic and copies ran while one was open for 0% of the time, Pallas kernels for 13%

commit v1 on v0

--- a/solution.py
+++ b/solution.py
@@ -12,6 +12,8 @@
 YS = 4
 EPSILON = 1e-06
 MASKED = -1e30
+MARK = 16
+TURNS = ((1, 1), (-1, -1), (2, 2))
 
 F32 = jnp.float32
 BF16 = jnp.bfloat16
@@ -36,6 +38,10 @@
     return values * lax.rsqrt(jnp.mean(values * values, axis=-1, keepdims=True) + EPSILON)
 
 
+def chunk_rows_at(start, multiple, rows):
+    return pl.ds(pl.multiple_of(start, multiple), rows)
+
+
 def chunk_rows(index, rows):
     return pl.ds(pl.multiple_of(index * rows, rows), rows)
 
@@ -44,8 +50,11 @@
     used = len(specs)
     specs = specs + [anywhere] * len(waits)
 
-    def body(*refs):
-        kernel(*refs[:used], *refs[used + len(waits) :])
+    def body(level, *refs):
+        frame = lax.axis_index("frame").astype(jnp.int32)
+        space = lax.axis_index("space").astype(jnp.int32)
+        info = (frame, space, frame // 2, frame % 2, level[0])
+        kernel(info, *refs[: used - 1], *refs[used - 1 + len(waits) :])
 
     return functools.partial(pallas(body, outs, specs, scratch, limit), waits)
 
@@ -98,8 +107,10 @@
     for copy in copies:
         copy.wait()
     level = levels_in[pl.ds(info[I_LEVEL], 1), :]
-    before = state_before(state_in[...], occupancy_in, embed[...], level)
+    before = state_before(state_in[...], occupancy_in, embed[...].reshape(1, -1), level)
     normed[...] = rms(before).astype(BF16)
+    size = normed.shape[0] // YS
+    chunks[1][size:, :] = jnp.full((MARK, normed.shape[1]), info[I_LEVEL], F32).astype(BF16)
     send_chunks(info, normed, chunks)
     pltpu.make_async_copy(reduce, piece, sems.at[3]).wait()
 
@@ -107,17 +118,23 @@
 def send_chunks(info, rows, chunks):
     size = rows.shape[0] // YS
     for k, chunk in enumerate(chunks):
-        chunk[...] = rows[chunk_rows(lax.rem(info[I_Y] + k, YS), size), :]
+        chunk[:size, :] = rows[chunk_rows(lax.rem(info[I_Y] + k, YS), size), :]
 
 
 def time_project_kernel(shift, info, c0, c1, c2, c3, project, queries, pairs, rows):
     size = c0.shape[0]
     for k, chunk in enumerate((c0, c1, c2, c3)):
         at = lax.rem(info[I_Y] + YS - k + shift * (YS - info[I_CORE]), YS)
-        rows[chunk_rows(at, size), :] = chunk[...]
+        rows[chunk_rows(at, size), :] = chunk[:size, :]
     width = rows.shape[1]
     values = rows[...]
-    pairs[...] = dot(values, project[:, width:]).astype(BF16)
+    count = values.shape[0]
+    pairs[:count, :] = dot(values, project[:, width:]).astype(BF16)
+    if pairs.shape[0] > count:
+        own = jnp.full((MARK, width), info[I_LEVEL], F32).astype(BF16)
+        mark = jnp.where(info[I_CORE] == 0, own, c1[size:, :])
+        pairs[count:, :width] = mark
+        pairs[count:, width:] = mark
     queries[...] = dot(values, project[:, :width]).astype(BF16)
 
 
@@ -183,7 +200,7 @@
     width = state.shape[1]
     count = state.shape[0]
     level = levels[pl.ds(info[I_LEVEL], 1), :]
-    before = state_before(state[...], occupied, embed[...], level)
+    before = state_before(state[...], occupied, embed[...].reshape(1, -1), level)
     own = rms(before).astype(BF16)
     scale = (width // HEADS) ** -0.5
     queries[...] = (dot(own, project[:, :width]).astype(BF16) * scale).astype(BF16)
@@ -233,58 +250,41 @@
 
 
 def finish_kernel(
-    hand_on, info, steps, next_level, state, occupied, embed, levels, space_term, m0, m1, m2, m3, output, *rest
+    hand_on, info, steps, state, occupied, embed, levels, space_term, m0, m1, m2, m3, output, *rest
 ):
-    weights = rest[:8]
-    if hand_on:
-        fresh, moved, normed = rest[8:11]
-        chunks = rest[11:15]
-        expand, reduce, mixed, sems = rest[15:]
-    else:
-        moved = rest[8]
-        expand, reduce, mixed, sems = rest[9:]
-    parts = len(weights) // 2
-    deep = weights[0].shape[0]
-
-    def copies(swap):
-        for i in range(parts):
-            first, second = (weights[parts + i], weights[i]) if swap else (weights[i], weights[parts + i])
-            part = pl.ds(i * deep, deep)
-            pltpu.make_async_copy(first, expand.at[part, :], sems.at[i]).start()
-            pltpu.make_async_copy(second, reduce.at[part, :], sems.at[parts + i]).start()
-
-    core = info[I_CORE]
-
-    @pl.when(core == 0)
-    def _():
-        copies(False)
-
-    @pl.when(core != 0)
-    def _():
-        copies(True)
-
+    weights, outs, mixed = rest[0], rest[1:-1], rest[-1]
     size = m0.shape[0]
     for k, chunk in enumerate((m0, m1, m2, m3)):
         mixed[chunk_rows(lax.rem(info[I_Y] + YS - k, YS), size), :] = chunk[...]
     level = levels[pl.ds(info[I_LEVEL], 1), :]
     current = state[...]
-    before = state_before(current, occupied, embed[...], level)
+    before = state_before(current, occupied, embed[...].reshape(1, -1), level)
     change = space_term[...] + dot(mixed[...], output[...])
     middle = rms(before + change).astype(BF16)
+    parts = len(TURNS) + 1
+    half = weights.shape[0] // 2
+    deep = half // parts
+    fine = deep // parts
+    expand = info[I_CORE] * half
+    reduce = half - expand
     for i in range(parts):
-        part = pl.ds(i * deep, deep)
-        pltpu.make_async_copy(weights[i], expand.at[part, :], sems.at[i]).wait()
-        pltpu.make_async_copy(weights[i], reduce.at[part, :], sems.at[parts + i]).wait()
-        hidden = jax.nn.gelu(dot_t(middle, expand[part, :]), approximate=True).astype(BF16)
-        change = change + dot(hidden, reduce[part, :])
+        matrix = weights[chunk_rows_at(expand + i * deep, fine, deep), :]
+        hidden = jax.nn.gelu(dot_t(middle, matrix), approximate=True).astype(BF16)
+        matrix = [
+            weights[chunk_rows_at(reduce + j * deep + i * fine, fine, fine), :] for j in range(parts)
+        ]
+        change = change + dot(hidden, jnp.concatenate(matrix, axis=0))
     result = (current.astype(F32) + steps[info[I_LEVEL]] * change).astype(BF16)
     if not hand_on:
-        moved[...] = result
+        outs[0][...] = result
         return
+    fresh, marked, moved, normed, *chunks = outs
     result = jnp.where(info[I_FRAME] == 0, fresh[...], result)
     moved[...] = result
-    level = levels[pl.ds(next_level[0], 1), :]
-    normed[...] = rms(state_before(result, occupied, embed[...], level)).astype(BF16)
+    number = marked[result.shape[0] :, :128].astype(F32)[:1, :1]
+    table = lax.broadcasted_iota(jnp.int32, levels.shape, 0).astype(F32)
+    level = jnp.sum(jnp.where(table == number, levels[...], 0.0), axis=0, keepdims=True)
+    normed[...] = rms(state_before(result, occupied, embed[...].reshape(1, -1), level)).astype(BF16)
     send_chunks(info, normed, chunks)
 
 
@@ -311,10 +311,6 @@
     frames = lax.axis_size("frame")
     spaces = lax.axis_size("space")
     xs, zs = 4, spaces // 4
-    frame = lax.axis_index("frame").astype(jnp.int32)
-    space = lax.axis_index("space").astype(jnp.int32)
-    core = frame % 2
-
     def along(block, axis, route):
         return lax.ppermute(block, axis, [(i, route(i)) for i in range(lax.axis_size(axis))])
 
@@ -329,22 +325,19 @@
     def y_on(f, k):
         return (f // 2 + k) % YS * 2 + f % 2
 
-    level_before = along(noise_levels, "frame", lambda f: (f + 1) % frames)
-    info = jnp.stack(
-        [frame, space, frame // 2, core, noise_levels[0]]
-    ).astype(jnp.int32)
+    info = noise_levels
     occupied = occupancy
-    embed = occupied_embed.reshape(1, width)
+    embed = occupied_embed
 
     def struct(*shape, dtype=BF16):
         return jax.ShapeDtypeStruct(shape, dtype)
 
     chunk_structs = [struct(chunk, width)] * YS
 
-    def attend(state, left, right, chunks, shift, waits):
+    def attend(state, left, right, chunks, shift, waits, between):
         queries, pairs = call(
             lambda *refs: time_project_kernel(shift, *refs),
-            [struct(rows, width), struct(rows, 2 * width)],
+            [struct(rows, width), struct(rows + (0 if shift else MARK), 2 * width)],
             [smem] + [vmem] * 5,
             [pltpu.VMEM((rows, width), BF16)],
             waits,
@@ -365,46 +358,47 @@
         mixed = [mixed[0]] + [
             along(mixed[k], "frame", lambda f, k=k: y_on(f, k)) for k in range(1, YS)
         ]
+        mixed, held = between(mixed)
         space_term = call(
             space_attend_kernel,
             struct(rows, width, dtype=F32),
             [smem] * 3 + [vmem] * 3,
             [pltpu.VMEM((rows, width), BF16)],
+            held,
         )(info, neighbors, brick_counts, space_queries, space_pairs, space_output)
-        return space_term, mixed
-
-    def finish(state, space_term, mixed, mine, other, hand_on):
-        hidden = 2 * sum(block.shape[0] for block in mine) // 2
-        specs = [smem, smem, smem] + [vmem] * 10 + [anywhere] * 8
-        operands = [info, step_size, level_before, state, occupied, embed, level_embed, space_term, *mixed]
-        operands += [time_output, *mine, *other]
+        return space_term, mixed, other_pairs
+
+    def finish(state, space_term, mixed, weights, marked, hand_on):
+        specs = [smem, smem] + [vmem] * 11
+        operands = [info, step_size, state, occupied, embed, level_embed, space_term, *mixed]
+        operands += [time_output, weights]
         outs = struct(rows, width)
         if hand_on:
-            specs.append(vmem)
-            operands.append(fresh_noise.reshape(rows, width))
+            specs += [vmem] * 2
+            operands += [fresh_noise.reshape(rows, width), marked]
             outs = [outs, outs] + chunk_structs
         return call(
             lambda *refs: finish_kernel(hand_on, *refs),
             outs,
             specs,
-            [
-                pltpu.VMEM((hidden, width), BF16),
-                pltpu.VMEM((hidden, width), BF16),
-                pltpu.VMEM((rows, width), BF16),
-                pltpu.SemaphoreType.DMA((8,)),
-            ],
+            [pltpu.VMEM((rows, width), BF16)],
         )(*operands)
 
-    def z_on(block, k):
-        return along(block, "space", lambda s: (s // xs + k) % zs * xs + s % xs)
-
-    def x_on(block, k):
-        return along(block, "space", lambda s: s // xs * xs + (s + k) % xs)
+    def z_step(k):
+        return lambda s: (s // xs + k) % zs * xs + s % xs
+
+    def x_step(k):
+        return lambda s: s // xs * xs + (s + k) % xs
+
+    def split(block, first, second):
+        return both(block, lambda f, s: (f, second(s) if f % 2 else first(s)))
 
     state = latents.reshape(rows, width)
     normed, piece, *chunks = call(
         pre_kernel,
-        [struct(rows, width), struct(reduce_weight.shape[0], width)] + chunk_structs,
+        [struct(rows, width), struct(reduce_weight.shape[0], width), chunk_structs[0]]
+        + [struct(chunk + MARK, width)]
+        + chunk_structs[2:],
         [smem] + [anywhere] * 3 + [vmem] + [anywhere] * 2,
         [
             pltpu.VMEM((rows, width), BF16),
@@ -414,7 +408,7 @@
         ],
         limit=60 * 1024 * 1024,
     )(info, state, occupancy, level_embed, embed, expand_weight.T, reduce_weight)
-    opposite = z_on(piece, zs // 2)
+    opposite = along(piece, "space", z_step(zs // 2))
     left = along(normed, "space", lambda s: (s + 1) % spaces)
     right = along(normed, "space", lambda s: (s - 1) % spaces)
     chunks = [chunks[0]] + [
@@ -423,23 +417,31 @@
     piece, opposite, left, right, *chunks = lax.optimization_barrier(
         (piece, opposite, left, right, *chunks)
     )
-    column = jnp.concatenate([piece, opposite], axis=0)
-    column = jnp.concatenate([column] + [z_on(column, k) for k in (1, 2, zs - 1)], axis=0)
-    mine = [column] + [x_on(column, k) for k in (1, 3, 2)]
-    space_term, mixed = attend(state, left, right, chunks, 0, [left, right])
+    part = jnp.concatenate([piece, opposite], axis=0)
+    column = jnp.concatenate(
+        [part] + [split(part, z_step(z), x_step(x)) for z, x in TURNS], axis=0
+    )
+    mine = [column] + [split(column, x_step(x), z_step(z)) for z, x in TURNS]
     other = [along(mine[0], "frame", lambda f: f ^ 1)]
-    space_term, *held = lax.optimization_barrier((space_term, *mixed, *mine[1:]))
-    mixed, arrived = held[:YS], held[YS:]
-    mine = [mine[0]] + arrived
-    other += [along(block, "frame", lambda f: f ^ 1) for block in arrived]
-    moved, normed, *chunks = finish(state, space_term, mixed, mine, other, True)
+
+    def exchange(mixed):
+        held = lax.optimization_barrier((*mixed, *mine[1:]))
+        mine[1:] = held[YS:]
+        other.extend(along(block, "frame", lambda f: f ^ 1) for block in mine[1:])
+        return held[:YS], [held[1]]
+
+    space_term, mixed, marked = attend(state, left, right, chunks, 0, [left, right], exchange)
+    weights = jnp.concatenate(mine + other, axis=0)
+    moved, normed, *chunks = finish(state, space_term, mixed, weights, marked, True)
 
     chunks = [along(chunks[k], "frame", lambda f, k=k: y_on(f ^ 1, k)) for k in range(YS)]
     state = along(moved, "frame", lambda f: (f - 1) % frames)
     left = both(normed, lambda f, s: ((f - 1) % frames, (s + 1) % spaces))
     right = both(normed, lambda f, s: ((f - 1) % frames, (s - 1) % spaces))
-    space_term, mixed = attend(state, left, right, chunks, 1, [state, left, right])
-    return finish(state, space_term, mixed, mine, other, False).reshape(1, blocks, brick, width)
+    space_term, mixed, _ = attend(
+        state, left, right, chunks, 1, [state, left, right], lambda mixed: (mixed, [])
+    )
+    return finish(state, space_term, mixed, weights, None, False).reshape(1, blocks, brick, width)
 
 
 def solution(mesh):

time: 108 us -> 99.5 us (0.921)
  Pallas kernels: 30.6 us -> 22.8 us
  waiting for transfers between devices: 18.5 us -> 14.8 us
  starting transfers between devices: 52.6 us -> 55.6 us
    ppermute x2 -> x8, starting transfers between devices: 6.22 us -> 15.3 us  [both(): return lax.ppermute(block, ('frame', 'space'), pairs)]
    pallas_call x11, Pallas kernels: 30.6 us -> 22.8 us  [pallas(): return lambda waits, *operands: made(*operands, *waits)]
    ppermute x30 -> x23, starting transfers between devices: 46.4 us -> 40.3 us  [along(): lax.ppermute(block, axis, [(i, route(i)) for i in range(lax.axis_size(axi...]
    ppermute x30 -> x23, waiting for transfers between devices: 18.5 us -> 14.8 us  [along(): lax.ppermute(block, axis, [(i, route(i)) for i in range(lax.axis_size(axi...]
    unnamed x33 -> x39, local copies, waits for them, and re-layouts: 2.99 us -> 4.94 us
    reshape x1 -> x0, local copies, waits for them, and re-layouts: 1.28 us -> none  [shards(): embed = occupied_embed.reshape(1, width)]
  transfers between devices with their start and end apart: 32 -> 31, of which waited for: 11 -> 9; matrix products, arithmetic and copies ran while one was open for 0% -> 0% of each run, Pallas kernels for 13% -> 12%
where the time goes in v1:
time: 99.5 us; the launch traced here: 99.2 us
  starting transfers between devices  55.6 us (56%)
  Pallas kernels  22.8 us (23%)
  waiting for transfers between devices  14.8 us (15%)
  local copies, waits for them, and re-layouts  4.98 us (5%)
  between operations  1.05 us (1%)
    ppermute x23, starting transfers between devices, along(): lax.ppermute(block, axis, [(i, route(i)) for i in range(lax.axis_size(axi...  40.3 us
    pallas_call x11, Pallas kernels, pallas(): return lambda waits, *operands: made(*operands, *waits)  22.8 us
    ppermute x8, starting transfers between devices, both(): return lax.ppermute(block, ('frame', 'space'), pairs)  15.3 us
    ppermute x23, waiting for transfers between devices, along(): lax.ppermute(block, axis, [(i, route(i)) for i in range(lax.axis_size(axi...  14.8 us
    unnamed x39, local copies, waits for them, and re-layouts  4.94 us
  transfers between devices with their start and end apart: 31, of which 9 were waited for; matrix products, arithmetic and copies ran while one was open for 0% of the time, Pallas kernels for 12%

profile of v1, /device:TPU:1, one launch (start us, length us, event | category | flops | bytes accessed | tf_op | source)
XLA Modules:
  0.0 99.2 jit_solution(18243731366049020681)
XLA Ops:
  0.7 2.7 %shard_map.145 = (bf16[128,768]{1,0:T(8,128)(2,1)}, bf16[48,768]{1,0:T(8,128)(2,1)}, bf16[32,768]{1,0:T(8,128)(2,1)}, bf16[48,768]{1,0:T(8,128)(2,1)}, bf16[32,768]{1,0:T(8,128)(2,1)}, /*index=5*/bf16[32,768]{1,0:T(8,128)(2,1)}) custom-call(s32[1]{0:T(128)S(6)} %copy.32.level, bf16[128,768]{1,0:T(8,128)(2,1)} %bitcast.4, s32[2,64]{1,0:T(2,128)} %refs_2_.9, ...), custom_call_target="tpu_custom_call" | custom-call | bytes 1 | tf_op jit(solution)/shard_map/pallas_call | solution.py:72
  3.5 2.1 %collective-permute-start.1 = (bf16[128,768]{1,0:T(8,128)(2,1)}, bf16[128,768]{1,0:T(8,128)(2,1)S(1)}, u32[]{:S(2)}, u32[]{:S(2)}) collective-permute-start(bf16[128,768]{1,0:T(8,128)(2,1)} %get-tuple-element.49), channel_id=1, source_target_pairs={{0,1},{1,2},{2,3},{3,4},{4,5},{5,6},{6,7},{7,8},{8,9},{9,10},{10,1... | collective-permute-start | bytes 589832 | tf_op jit(solution)/shard_map/ppermute | solution.py:315
  5.6 6.6 %collective-permute-start.2 = (bf16[128,768]{1,0:T(8,128)(2,1)}, bf16[128,768]{1,0:T(8,128)(2,1)S(1)}, u32[]{:S(2)}, u32[]{:S(2)}) collective-permute-start(bf16[128,768]{1,0:T(8,128)(2,1)} %get-tuple-element.49), channel_id=1, source_target_pairs={{0,31},{1,0},{2,1},{3,2},{4,3},{5,4},{6,5},{7,6},{8,7},{9,8},{10,9... | collective-permute-start | bytes 589832 | tf_op jit(solution)/shard_map/ppermute | solution.py:315
  12.2 2.9 %collective-permute-start.4 = (bf16[32,768]{1,0:T(8,128)(2,1)}, bf16[32,768]{1,0:T(8,128)(2,1)S(1)}, u32[]{:S(2)}, u32[]{:S(2)}) collective-permute-start(bf16[32,768]{1,0:T(8,128)(2,1)} %get-tuple-element.52), channel_id=1, source_target_pairs={{0,128},{32,160},{64,192},{96,224},{128,0},{160,32},{192,64},{224,... | collective-permute-start | bytes 147464 | tf_op jit(solution)/shard_map/ppermute | solution.py:315
  15.1 3.8 %collective-permute-start = (bf16[48,768]{1,0:T(8,128)(2,1)}, bf16[48,768]{1,0:T(8,128)(2,1)S(1)}, u32[]{:S(2)}, u32[]{:S(2)}) collective-permute-start(bf16[48,768]{1,0:T(8,128)(2,1)} %get-tuple-element.68), channel_id=1, source_target_pairs={{0,16},{1,17},{2,18},{3,19},{4,20},{5,21},{6,22},{7,23},{8,24},{9,... | collective-permute-start | bytes 221192 | tf_op jit(solution)/shard_map/ppermute | solution.py:315
  19.4 2.3 %collective-permute-start.5 = (bf16[32,768]{1,0:T(8,128)(2,1)}, bf16[32,768]{1,0:T(8,128)(2,1)S(1)}, u32[]{:S(2)}, u32[]{:S(2)}) collective-permute-start(bf16[32,768]{1,0:T(8,128)(2,1)} %get-tuple-element.53), channel_id=1, source_target_pairs={{0,192},{32,224},{64,0},{96,32},{128,64},{160,96},{192,128},{224,1... | collective-permute-start | bytes 147464 | tf_op jit(solution)/shard_map/ppermute | solution.py:315
  24.9 2.7 %collective-permute-start.11 = (bf16[96,768]{1,0:T(8,128)(2,1)S(1)}, bf16[96,768]{1,0:T(8,128)(2,1)S(1)}, u32[]{:S(2)}, u32[]{:S(2)}) collective-permute-start(bf16[96,768]{1,0:T(8,128)(2,1)S(1)} %get-tuple-element.99), channel_id=1, source_target_pairs={{0,28},{1,29},{2,30},{3,31},{4,0},{5,1},{6,2},{7,3},{8,4},{9,5},{1... | collective-permute-start | bytes 442376 | tf_op jit(solution)/shard_map/ppermute | solution.py:323
  27.6 2.0 %copy-done = bf16[768,2304]{1,0:T(8,128)(2,1)S(1)} copy-done((bf16[768,2304]{1,0:T(8,128)(2,1)S(1)}, bf16[768,2304]{1,0:T(8,128)(2,1)}, u32[]{:S(2)}) %copy-start) | copy-done | bytes 3538968
  31.1 3.3 %collective-permute-start.6 = (bf16[144,1536]{1,0:T(8,128)(2,1)S(1)}, bf16[144,1536]{1,0:T(8,128)(2,1)S(1)}, u32[]{:S(2)}, u32[]{:S(2)}) collective-permute-start(bf16[144,1536]{1,0:T(8,128)(2,1)S(1)} %get-tuple-element.63.refs_1_), channel_id=1, source_target_pairs={{0,32},{32,0},{64,96},{96,64},{128,160},{160,128},{192,224},{224,1... | collective-permute-start | bytes 1327112 | tf_op jit(solution)/shard_map/ppermute | solution.py:315
  34.9 2.4 %collective-permute-start.14 = (bf16[384,768]{1,0:T(8,128)(2,1)S(1)}, bf16[384,768]{1,0:T(8,128)(2,1)S(1)}, u32[]{:S(2)}, u32[]{:S(2)}) collective-permute-start(bf16[384,768]{1,0:T(8,128)(2,1)S(1)} %get-tuple-element.92), channel_id=1, source_target_pairs={{0,3},{1,0},{2,1},{3,2},{4,7},{5,4},{6,5},{7,6},{8,11},{9,8},{10,9... | collective-permute-start | bytes 1769480 | tf_op jit(solution)/shard_map/ppermute | solution.py:323
  37.2 1.8 %collective-permute-start.15 = (bf16[384,768]{1,0:T(8,128)(2,1)S(1)}, bf16[384,768]{1,0:T(8,128)(2,1)S(1)}, u32[]{:S(2)}, u32[]{:S(2)}) collective-permute-start(bf16[384,768]{1,0:T(8,128)(2,1)S(1)} %get-tuple-element.92), channel_id=1, source_target_pairs={{0,2},{1,3},{2,0},{3,1},{4,6},{5,7},{6,4},{7,5},{8,10},{9,11},{10,... | collective-permute-start | bytes 1769480 | tf_op jit(solution)/shard_map/ppermute | solution.py:323
  42.3 3.0 %collective-permute-start.16 = (bf16[384,768]{1,0:T(8,128)(2,1)S(1)}, bf16[384,768]{1,0:T(8,128)(2,1)S(1)}, u32[]{:S(2)}, u32[]{:S(2)}) collective-permute-start(bf16[384,768]{1,0:T(8,128)(2,1)S(1)} %get-tuple-element.92), channel_id=1, source_target_pairs={{0,32},{32,0},{64,96},{96,64},{128,160},{160,128},{192,224},{224,1... | collective-permute-start | bytes 1769480 | tf_op jit(solution)/shard_map/ppermute | solution.py:315
  46.3 3.0 %collective-permute-start.8 = (bf16[32,768]{1,0:T(8,128)(2,1)S(1)}, bf16[32,768]{1,0:T(8,128)(2,1)S(1)}, u32[]{:S(2)}, u32[]{:S(2)}) collective-permute-start(bf16[32,768]{1,0:T(8,128)(2,1)S(1)} %get-tuple-element.66), channel_id=1, source_target_pairs={{0,128},{32,160},{64,192},{96,224},{128,0},{160,32},{192,64},{224,... | collective-permute-start | bytes 147464 | tf_op jit(solution)/shard_map/ppermute | solution.py:315
  49.3 2.1 %collective-permute-done.8.refs_8_ = bf16[32,768]{1,0:T(8,128)(2,1)S(1)} collective-permute-done((bf16[32,768]{1,0:T(8,128)(2,1)S(1)}, bf16[32,768]{1,0:T(8,128)(2,1)S(1)}, u32[]{:S(2)}, u32[]{:S(2)}) %collective-permute-start.8) | collective-permute-done | bytes 49184 | tf_op jit(solution)/shard_map/ppermute | solution.py:315
  52.9 2.0 %collective-permute-done.9.refs_9_ = bf16[32,768]{1,0:T(8,128)(2,1)S(1)} collective-permute-done((bf16[32,768]{1,0:T(8,128)(2,1)S(1)}, bf16[32,768]{1,0:T(8,128)(2,1)S(1)}, u32[]{:S(2)}, u32[]{:S(2)}) %collective-permute-start.9) | collective-permute-done | bytes 49184 | tf_op jit(solution)/shard_map/ppermute | solution.py:315
  54.9 5.3 %collective-permute-start.17 = (bf16[384,768]{1,0:T(8,128)(2,1)S(1)}, bf16[384,768]{1,0:T(8,128)(2,1)S(1)}, u32[]{:S(2)}, u32[]{:S(2)}) collective-permute-start(bf16[384,768]{1,0:T(8,128)(2,1)S(1)} %collective-permute-done.13), channel_id=1, source_target_pairs={{0,32},{32,0},{64,96},{96,64},{128,160},{160,128},{192,224},{224,1... | collective-permute-start | bytes 1769480 | tf_op jit(solution)/shard_map/ppermute | solution.py:315
  60.8 3.4 %shard_map.149.refs_5_ = f32[128,768]{1,0:T(8,128)S(1)} custom-call(s32[1]{0:T(128)S(6)} %copy.32.level, s32[2,6]{1,0:T(2,128)S(1)} %copy-done.11, s32[64]{0:T(128)S(1)} %copy-done.12, bf16[128,768]{1,0:T(8,128)(2,1)S(1)} %get-tuple-element.56.refs_3_.refs_2_, bf16[384,1536]{1,0:T(8,128)(2,1)S(1)} %get-tuple-element.57.refs_3_, ...), custom_call_target="tpu_custom_call" | custom-call | bytes 1 | tf_op jit(solution)/shard_map/pallas_call | solution.py:72
  65.5 3.0 %shard_map.150 = (bf16[128,768]{1,0:T(8,128)(2,1)S(1)}, bf16[128,768]{1,0:T(8,128)(2,1)S(1)}, bf16[32,768]{1,0:T(8,128)(2,1)S(1)}, bf16[32,768]{1,0:T(8,128)(2,1...) custom-call(s32[1]{0:T(128)S(6)} %copy.32.level, f32[16]{0:T(128)S(1)} %copy-done.13, ...), custom_call_target="tpu_custom_call" | custom-call | bytes 1 | tf_op jit(solution)/shard_map/pallas_call | solution.py:72
  68.6 3.8 %collective-permute-start.21 = (bf16[128,768]{1,0:T(8,128)(2,1)S(1)}, bf16[128,768]{1,0:T(8,128)(2,1)S(1)}, u32[]{:S(2)}, u32[]{:S(2)}) collective-permute-start(bf16[128,768]{1,0:T(8,128)(2,1)S(1)} %get-tuple-element.78), channel_id=1, source_target_pairs={{0,225},{1,226},{2,227},{3,228},{4,229},{5,230},{6,231},{7,232},{8... | collective-permute-start | bytes 589832 | tf_op jit(solution)/shard_map/ppermute | solution.py:323
  72.4 4.2 %collective-permute-start.22 = (bf16[128,768]{1,0:T(8,128)(2,1)S(1)}, bf16[128,768]{1,0:T(8,128)(2,1)S(1)}, u32[]{:S(2)}, u32[]{:S(2)}) collective-permute-start(bf16[128,768]{1,0:T(8,128)(2,1)S(1)} %get-tuple-element.78), channel_id=1, source_target_pairs={{0,255},{1,224},{2,225},{3,226},{4,227},{5,228},{6,229},{7,230},{8... | collective-permute-start | bytes 589832 | tf_op jit(solution)/shard_map/ppermute | solution.py:323
  78.2 3.7 %collective-permute-done.24.refs_1_ = bf16[32,768]{1,0:T(8,128)(2,1)S(1)} collective-permute-done((bf16[32,768]{1,0:T(8,128)(2,1)S(1)}, bf16[32,768]{1,0:T(8,128)(2,1)S(1)}, u32[]{:S(2)}, u32[]{:S(2)}) %collective-permute-start.24) | collective-permute-done | bytes 49184 | tf_op jit(solution)/shard_map/ppermute | solution.py:315
  89.5 2.1 %collective-permute-start.29 = (bf16[32,768]{1,0:T(8,128)(2,1)S(1)}, bf16[32,768]{1,0:T(8,128)(2,1)S(1)}, u32[]{:S(2)}, u32[]{:S(2)}) collective-permute-start(bf16[32,768]{1,0:T(8,128)(2,1)S(1)} %get-tuple-element.89), channel_id=1, source_target_pairs={{0,128},{32,160},{64,192},{96,224},{128,0},{160,32},{192,64},{224,... | collective-permute-start | bytes 147464 | tf_op jit(solution)/shard_map/ppermute | solution.py:315
  92.2 3.4 %shard_map.152.refs_5_ = f32[128,768]{1,0:T(8,128)S(1)} custom-call(s32[1]{0:T(128)S(6)} %copy.32.level, s32[2,6]{1,0:T(2,128)S(1)} %copy-done.11, s32[64]{0:T(128)S(1)} %copy-done.12, bf16[128,768]{1,0:T(8,128)(2,1)S(1)} %get-tuple-element.79.refs_2_.refs_3_, bf16[384,1536]{1,0:T(8,128)(2,1)S(1)} %get-tuple-element.80.refs_3_, bf16[768,768]{1,0:T(8,128)(2,1)S(1)} %copy-done.3), custom_call_target="tpu_custom_call" | custom-call | bytes 1 | tf_op jit(solution)/shard_map/pallas_call | solution.py:72
  95.7 3.5 %shard_map.155 = bf16[128,768]{1,0:T(8,128)(2,1)} custom-call(s32[1]{0:T(128)S(6)} %copy.32.level, f32[16]{0:T(128)S(1)} %copy-done.13, bf16[128,768]{1,0:T(8,128)(2,1)S(1)} %collective-permute-done.20.refs_0_.refs_5_.refs_1_, s32[2,64]{1,0:T(2,128)S(1)} %copy-done.10, f32[768]{0:T(1024)S(1)} %copy-done.8, f32[16,768]{1,0:T(8,128)S(1)} %copy-done.6, ...), custom_call_target="tpu_custom_call" | custom-call | bytes 1 | tf_op jit(solution)/shard_map/pallas_call | solution.py:72
  (89 shorter events, 22.9 us)
Async XLA Ops:
  3.5 20.4 %collective-permute-start.1 = (bf16[128,768]{1,0:T(8,128)(2,1)}, bf16[128,768]{1,0:T(8,128)(2,1)S(1)}, u32[]{:S(2)}, u32[]{:S(2)}) collective-permute-start(bf16[128,768]{1,0:T(8,128)(2,1)} %get-tuple-element.49), channel_id=1, source_target_pairs={{0,1},{1,2},{2,3},{3,4},{4,5},{5,6},{6,7},{7,8},{8,9},{9,10},{10,1... | collective-permute-start | bytes 589832 | tf_op jit(solution)/shard_map/ppermute | solution.py:315
  5.6 18.3 %collective-permute-start.2 = (bf16[128,768]{1,0:T(8,128)(2,1)}, bf16[128,768]{1,0:T(8,128)(2,1)S(1)}, u32[]{:S(2)}, u32[]{:S(2)}) collective-permute-start(bf16[128,768]{1,0:T(8,128)(2,1)} %get-tuple-element.49), channel_id=1, source_target_pairs={{0,31},{1,0},{2,1},{3,2},{4,3},{5,4},{6,5},{7,6},{8,7},{9,8},{10,9... | collective-permute-start | bytes 589832 | tf_op jit(solution)/shard_map/ppermute | solution.py:315
  12.2 7.2 %collective-permute-start.4 = (bf16[32,768]{1,0:T(8,128)(2,1)}, bf16[32,768]{1,0:T(8,128)(2,1)S(1)}, u32[]{:S(2)}, u32[]{:S(2)}) collective-permute-start(bf16[32,768]{1,0:T(8,128)(2,1)} %get-tuple-element.52), channel_id=1, source_target_pairs={{0,128},{32,160},{64,192},{96,224},{128,0},{160,32},{192,64},{224,... | collective-permute-start | bytes 147464 | tf_op jit(solution)/shard_map/ppermute | solution.py:315
  15.1 8.0 %collective-permute-start = (bf16[48,768]{1,0:T(8,128)(2,1)}, bf16[48,768]{1,0:T(8,128)(2,1)S(1)}, u32[]{:S(2)}, u32[]{:S(2)}) collective-permute-start(bf16[48,768]{1,0:T(8,128)(2,1)} %get-tuple-element.68), channel_id=1, source_target_pairs={{0,16},{1,17},{2,18},{3,19},{4,20},{5,21},{6,22},{7,23},{8,24},{9,... | collective-permute-start | bytes 221192 | tf_op jit(solution)/shard_map/ppermute | solution.py:315
  19.0 4.9 %collective-permute-start.3 = (bf16[48,768]{1,0:T(8,128)(2,1)}, bf16[48,768]{1,0:T(8,128)(2,1)S(1)}, u32[]{:S(2)}, u32[]{:S(2)}) collective-permute-start(bf16[48,768]{1,0:T(8,128)(2,1)} %get-tuple-element.51), channel_id=1, source_target_pairs={{0,64},{32,96},{64,128},{96,160},{128,192},{160,224},{192,0},{224,... | collective-permute-start | bytes 221192 | tf_op jit(solution)/shard_map/ppermute | solution.py:315
  24.9 9.5 %collective-permute-start.10 = (bf16[96,768]{1,0:T(8,128)(2,1)S(1)}, bf16[96,768]{1,0:T(8,128)(2,1)S(1)}, u32[]{:S(2)}, u32[]{:S(2)}) collective-permute-start(bf16[96,768]{1,0:T(8,128)(2,1)S(1)} %get-tuple-element.99), channel_id=1, source_target_pairs={{0,4},{1,5},{2,6},{3,7},{4,8},{5,9},{6,10},{7,11},{8,12},{9,13},{1... | collective-permute-start | bytes 442376 | tf_op jit(solution)/shard_map/ppermute | solution.py:323
  24.9 9.5 %collective-permute-start.11 = (bf16[96,768]{1,0:T(8,128)(2,1)S(1)}, bf16[96,768]{1,0:T(8,128)(2,1)S(1)}, u32[]{:S(2)}, u32[]{:S(2)}) collective-permute-start(bf16[96,768]{1,0:T(8,128)(2,1)S(1)} %get-tuple-element.99), channel_id=1, source_target_pairs={{0,28},{1,29},{2,30},{3,31},{4,0},{5,1},{6,2},{7,3},{8,4},{9,5},{1... | collective-permute-start | bytes 442376 | tf_op jit(solution)/shard_map/ppermute | solution.py:323
  27.6 6.8 %collective-permute-start.12 = (bf16[96,768]{1,0:T(8,128)(2,1)S(1)}, bf16[96,768]{1,0:T(8,128)(2,1)S(1)}, u32[]{:S(2)}, u32[]{:S(2)}) collective-permute-start(bf16[96,768]{1,0:T(8,128)(2,1)S(1)} %get-tuple-element.99), channel_id=1, source_target_pairs={{0,8},{1,9},{2,10},{3,11},{4,12},{5,13},{6,14},{7,15},{8,16},{9,17... | collective-permute-start | bytes 442376 | tf_op jit(solution)/shard_map/ppermute | solution.py:323
  31.1 9.5 %collective-permute-start.6 = (bf16[144,1536]{1,0:T(8,128)(2,1)S(1)}, bf16[144,1536]{1,0:T(8,128)(2,1)S(1)}, u32[]{:S(2)}, u32[]{:S(2)}) collective-permute-start(bf16[144,1536]{1,0:T(8,128)(2,1)S(1)} %get-tuple-element.63.refs_1_), channel_id=1, source_target_pairs={{0,32},{32,0},{64,96},{96,64},{128,160},{160,128},{192,224},{224,1... | collective-permute-start | bytes 1327112 | tf_op jit(solution)/shard_map/ppermute | solution.py:315
  34.5 20.4 %collective-permute-start.13 = (bf16[384,768]{1,0:T(8,128)(2,1)S(1)}, bf16[384,768]{1,0:T(8,128)(2,1)S(1)}, u32[]{:S(2)}, u32[]{:S(2)}) collective-permute-start(bf16[384,768]{1,0:T(8,128)(2,1)S(1)} %get-tuple-element.92), channel_id=1, source_target_pairs={{0,1},{1,2},{2,3},{3,0},{4,5},{5,6},{6,7},{7,4},{8,9},{9,10},{10,1... | collective-permute-start | bytes 1769480 | tf_op jit(solution)/shard_map/ppermute | solution.py:323
  34.9 20.0 %collective-permute-start.14 = (bf16[384,768]{1,0:T(8,128)(2,1)S(1)}, bf16[384,768]{1,0:T(8,128)(2,1)S(1)}, u32[]{:S(2)}, u32[]{:S(2)}) collective-permute-start(bf16[384,768]{1,0:T(8,128)(2,1)S(1)} %get-tuple-element.92), channel_id=1, source_target_pairs={{0,3},{1,0},{2,1},{3,2},{4,7},{5,4},{6,5},{7,6},{8,11},{9,8},{10,9... | collective-permute-start | bytes 1769480 | tf_op jit(solution)/shard_map/ppermute | solution.py:323
  37.2 17.6 %collective-permute-start.15 = (bf16[384,768]{1,0:T(8,128)(2,1)S(1)}, bf16[384,768]{1,0:T(8,128)(2,1)S(1)}, u32[]{:S(2)}, u32[]{:S(2)}) collective-permute-start(bf16[384,768]{1,0:T(8,128)(2,1)S(1)} %get-tuple-element.92), channel_id=1, source_target_pairs={{0,2},{1,3},{2,0},{3,1},{4,6},{5,7},{6,4},{7,5},{8,10},{9,11},{10,... | collective-permute-start | bytes 1769480 | tf_op jit(solution)/shard_map/ppermute | solution.py:323
  41.8 4.5 %collective-permute-start.7 = (bf16[32,768]{1,0:T(8,128)(2,1)S(1)}, bf16[32,768]{1,0:T(8,128)(2,1)S(1)}, u32[]{:S(2)}, u32[]{:S(2)}) collective-permute-start(bf16[32,768]{1,0:T(8,128)(2,1)S(1)} %get-tuple-element.65), channel_id=1, source_target_pairs={{0,64},{32,96},{64,128},{96,160},{128,192},{160,224},{192,0},{224,... | collective-permute-start | bytes 147464 | tf_op jit(solution)/shard_map/ppermute | solution.py:315
  42.3 22.1 %collective-permute-start.16 = (bf16[384,768]{1,0:T(8,128)(2,1)S(1)}, bf16[384,768]{1,0:T(8,128)(2,1)S(1)}, u32[]{:S(2)}, u32[]{:S(2)}) collective-permute-start(bf16[384,768]{1,0:T(8,128)(2,1)S(1)} %get-tuple-element.92), channel_id=1, source_target_pairs={{0,32},{32,0},{64,96},{96,64},{128,160},{160,128},{192,224},{224,1... | collective-permute-start | bytes 1769480 | tf_op jit(solution)/shard_map/ppermute | solution.py:315
  46.3 5.2 %collective-permute-start.8 = (bf16[32,768]{1,0:T(8,128)(2,1)S(1)}, bf16[32,768]{1,0:T(8,128)(2,1)S(1)}, u32[]{:S(2)}, u32[]{:S(2)}) collective-permute-start(bf16[32,768]{1,0:T(8,128)(2,1)S(1)} %get-tuple-element.66), channel_id=1, source_target_pairs={{0,128},{32,160},{64,192},{96,224},{128,0},{160,32},{192,64},{224,... | collective-permute-start | bytes 147464 | tf_op jit(solution)/shard_map/ppermute | solution.py:315
  54.9 9.6 %collective-permute-start.17 = (bf16[384,768]{1,0:T(8,128)(2,1)S(1)}, bf16[384,768]{1,0:T(8,128)(2,1)S(1)}, u32[]{:S(2)}, u32[]{:S(2)}) collective-permute-start(bf16[384,768]{1,0:T(8,128)(2,1)S(1)} %collective-permute-done.13), channel_id=1, source_target_pairs={{0,32},{32,0},{64,96},{96,64},{128,160},{160,128},{192,224},{224,1... | collective-permute-start | bytes 1769480 | tf_op jit(solution)/shard_map/ppermute | solution.py:315
  60.2 4.3 %collective-permute-start.18 = (bf16[384,768]{1,0:T(8,128)(2,1)S(1)}, bf16[384,768]{1,0:T(8,128)(2,1)S(1)}, u32[]{:S(2)}, u32[]{:S(2)}) collective-permute-start(bf16[384,768]{1,0:T(8,128)(2,1)S(1)} %collective-permute-done.14), channel_id=1, source_target_pairs={{0,32},{32,0},{64,96},{96,64},{128,160},{160,128},{192,224},{224,1... | collective-permute-start | bytes 1769480 | tf_op jit(solution)/shard_map/ppermute | solution.py:315
  68.5 17.0 %collective-permute-start.20 = (bf16[128,768]{1,0:T(8,128)(2,1)S(1)}, bf16[128,768]{1,0:T(8,128)(2,1)S(1)}, u32[]{:S(2)}, u32[]{:S(2)}) collective-permute-start(bf16[128,768]{1,0:T(8,128)(2,1)S(1)} %get-tuple-element.77), channel_id=1, source_target_pairs={{0,224},{32,0},{64,32},{96,64},{128,96},{160,128},{192,160},{224,1... | collective-permute-start | bytes 589832 | tf_op jit(solution)/shard_map/ppermute | solution.py:315
  68.6 16.9 %collective-permute-start.21 = (bf16[128,768]{1,0:T(8,128)(2,1)S(1)}, bf16[128,768]{1,0:T(8,128)(2,1)S(1)}, u32[]{:S(2)}, u32[]{:S(2)}) collective-permute-start(bf16[128,768]{1,0:T(8,128)(2,1)S(1)} %get-tuple-element.78), channel_id=1, source_target_pairs={{0,225},{1,226},{2,227},{3,228},{4,229},{5,230},{6,231},{7,232},{8... | collective-permute-start | bytes 589832 | tf_op jit(solution)/shard_map/ppermute | solution.py:323
  72.4 13.1 %collective-permute-start.22 = (bf16[128,768]{1,0:T(8,128)(2,1)S(1)}, bf16[128,768]{1,0:T(8,128)(2,1)S(1)}, u32[]{:S(2)}, u32[]{:S(2)}) collective-permute-start(bf16[128,768]{1,0:T(8,128)(2,1)S(1)} %get-tuple-element.78), channel_id=1, source_target_pairs={{0,255},{1,224},{2,225},{3,226},{4,227},{5,228},{6,229},{7,230},{8... | collective-permute-start | bytes 589832 | tf_op jit(solution)/shard_map/ppermute | solution.py:323
  76.7 5.3 %collective-permute-start.24 = (bf16[32,768]{1,0:T(8,128)(2,1)S(1)}, bf16[32,768]{1,0:T(8,128)(2,1)S(1)}, u32[]{:S(2)}, u32[]{:S(2)}) collective-permute-start(bf16[32,768]{1,0:T(8,128)(2,1)S(1)} %get-tuple-element.82), channel_id=1, source_target_pairs={{0,96},{32,64},{64,160},{96,128},{128,224},{160,192},{192,32},{224... | collective-permute-start | bytes 147464 | tf_op jit(solution)/shard_map/ppermute | solution.py:315
  78.2 5.5 %collective-permute-start.25 = (bf16[32,768]{1,0:T(8,128)(2,1)S(1)}, bf16[32,768]{1,0:T(8,128)(2,1)S(1)}, u32[]{:S(2)}, u32[]{:S(2)}) collective-permute-start(bf16[32,768]{1,0:T(8,128)(2,1)S(1)} %get-tuple-element.83), channel_id=1, source_target_pairs={{0,160},{32,128},{64,224},{96,192},{128,32},{160,0},{192,96},{224,... | collective-permute-start | bytes 147464 | tf_op jit(solution)/shard_map/ppermute | solution.py:315
  89.2 6.5 %collective-permute-start.28 = (bf16[32,768]{1,0:T(8,128)(2,1)S(1)}, bf16[32,768]{1,0:T(8,128)(2,1)S(1)}, u32[]{:S(2)}, u32[]{:S(2)}) collective-permute-start(bf16[32,768]{1,0:T(8,128)(2,1)S(1)} %get-tuple-element.88), channel_id=1, source_target_pairs={{0,64},{32,96},{64,128},{96,160},{128,192},{160,224},{192,0},{224,... | collective-permute-start | bytes 147464 | tf_op jit(solution)/shard_map/ppermute | solution.py:315
  89.5 6.2 %collective-permute-start.29 = (bf16[32,768]{1,0:T(8,128)(2,1)S(1)}, bf16[32,768]{1,0:T(8,128)(2,1)S(1)}, u32[]{:S(2)}, u32[]{:S(2)}) collective-permute-start(bf16[32,768]{1,0:T(8,128)(2,1)S(1)} %get-tuple-element.89), channel_id=1, source_target_pairs={{0,128},{32,160},{64,192},{96,224},{128,0},{160,32},{192,64},{224,... | collective-permute-start | bytes 147464 | tf_op jit(solution)/shard_map/ppermute | solution.py:315
  (21 other events, 316.9 us)

commit v2 on v1

--- a/solution.py
+++ b/solution.py
@@ -334,14 +334,16 @@
 
     chunk_structs = [struct(chunk, width)] * YS
 
-    def attend(state, left, right, chunks, shift, waits, between):
-        queries, pairs = call(
+    def project(chunks, shift, waits):
+        return call(
             lambda *refs: time_project_kernel(shift, *refs),
             [struct(rows, width), struct(rows + (0 if shift else MARK), 2 * width)],
             [smem] + [vmem] * 5,
             [pltpu.VMEM((rows, width), BF16)],
             waits,
         )(info, *chunks, time_project)
+
+    def attend(state, left, right, queries, pairs, between):
         other_pairs = along(pairs, "frame", lambda f: f ^ 1)
         space_queries, space_pairs = call(
             space_project_kernel,
@@ -421,16 +423,19 @@
     column = jnp.concatenate(
         [part] + [split(part, z_step(z), x_step(x)) for z, x in TURNS], axis=0
     )
+    queries, pairs, column = lax.optimization_barrier(
+        (*project(chunks, 0, [left, right]), column)
+    )
     mine = [column] + [split(column, x_step(x), z_step(z)) for z, x in TURNS]
-    other = [along(mine[0], "frame", lambda f: f ^ 1)]
+    other = []
 
     def exchange(mixed):
-        held = lax.optimization_barrier((*mixed, *mine[1:]))
-        mine[1:] = held[YS:]
-        other.extend(along(block, "frame", lambda f: f ^ 1) for block in mine[1:])
+        held = lax.optimization_barrier((*mixed, *mine))
+        mine[:] = held[YS:]
+        other.extend(along(block, "frame", lambda f: f ^ 1) for block in mine)
         return held[:YS], [held[1]]
 
-    space_term, mixed, marked = attend(state, left, right, chunks, 0, [left, right], exchange)
+    space_term, mixed, marked = attend(state, left, right, queries, pairs, exchange)
     weights = jnp.concatenate(mine + other, axis=0)
     moved, normed, *chunks = finish(state, space_term, mixed, weights, marked, True)
 
@@ -438,8 +443,9 @@
     state = along(moved, "frame", lambda f: (f - 1) % frames)
     left = both(normed, lambda f, s: ((f - 1) % frames, (s + 1) % spaces))
     right = both(normed, lambda f, s: ((f - 1) % frames, (s - 1) % spaces))
+    queries, pairs = project(chunks, 1, [state, left, right])
     space_term, mixed, _ = attend(
-        state, left, right, chunks, 1, [state, left, right], lambda mixed: (mixed, [])
+        state, left, right, queries, pairs, lambda mixed: (mixed, [])
     )
     return finish(state, space_term, mixed, weights, None, False).reshape(1, blocks, brick, width)
 

time: 99.5 us -> 97.3 us (0.978)
  starting transfers between devices: 55.6 us -> 51.6 us
  waiting for transfers between devices: 14.8 us -> 16.7 us
    ppermute x8, waiting for transfers between devices: 0.02 us -> 4.28 us  [both(): return lax.ppermute(block, ('frame', 'space'), pairs)]
    ppermute x23, waiting for transfers between devices: 14.8 us -> 12.4 us  [along(): lax.ppermute(block, axis, [(i, route(i)) for i in range(lax.axis_size(axi...]
    ppermute x8, starting transfers between devices: 15.3 us -> 13.2 us  [both(): return lax.ppermute(block, ('frame', 'space'), pairs)]
    ppermute x23, starting transfers between devices: 40.3 us -> 38.3 us  [along(): lax.ppermute(block, axis, [(i, route(i)) for i in range(lax.axis_size(axi...]
    unnamed x39 -> x38, local copies, waits for them, and re-layouts: 4.94 us -> 4.86 us
  transfers between devices with their start and end apart: 31 -> 31, of which waited for: 9 -> 11; matrix products, arithmetic and copies ran while one was open for 0% -> 0% of each run, Pallas kernels for 12% -> 12%
where the time goes in v2:
time: 97.3 us; the launch traced here: 97.1 us
  starting transfers between devices  51.6 us (53%)
  Pallas kernels  22.8 us (23%)
  waiting for transfers between devices  16.7 us (17%)
  local copies, waits for them, and re-layouts  4.93 us (5%)
  between operations  1.07 us (1%)
    ppermute x23, starting transfers between devices, along(): lax.ppermute(block, axis, [(i, route(i)) for i in range(lax.axis_size(axi...  38.3 us
    pallas_call x11, Pallas kernels, pallas(): return lambda waits, *operands: made(*operands, *waits)  22.8 us
    ppermute x8, starting transfers between devices, both(): return lax.ppermute(block, ('frame', 'space'), pairs)  13.2 us
    ppermute x23, waiting for transfers between devices, along(): lax.ppermute(block, axis, [(i, route(i)) for i in range(lax.axis_size(axi...  12.4 us
    unnamed x38, local copies, waits for them, and re-layouts  4.86 us
    ppermute x8, waiting for transfers between devices, both(): return lax.ppermute(block, ('frame', 'space'), pairs)  4.28 us
  transfers between devices with their start and end apart: 31, of which 11 were waited for; matrix products, arithmetic and copies ran while one was open for 0% of the time, Pallas kernels for 12%

profile of v2, /device:TPU:1, one launch (start us, length us, event | category | flops | bytes accessed | tf_op | source)
XLA Modules:
  0.0 97.1 jit_solution(17116657983295808032)
XLA Ops:
  0.7 2.7 %shard_map.145 = (bf16[128,768]{1,0:T(8,128)(2,1)}, bf16[48,768]{1,0:T(8,128)(2,1)}, bf16[32,768]{1,0:T(8,128)(2,1)}, bf16[48,768]{1,0:T(8,128)(2,1)}, bf16[32,768]{1,0:T(8,128)(2,1)}, /*index=5*/bf16[32,768]{1,0:T(8,128)(2,1)}) custom-call(s32[1]{0:T(128)S(6)} %copy.28.level, bf16[128,768]{1,0:T(8,128)(2,1)} %bitcast.4, s32[2,64]{1,0:T(2,128)} %refs_2_.9, ...), custom_call_target="tpu_custom_call" | custom-call | bytes 1 | tf_op jit(solution)/shard_map/pallas_call | solution.py:72
  3.5 2.1 %collective-permute-start.1 = (bf16[128,768]{1,0:T(8,128)(2,1)}, bf16[128,768]{1,0:T(8,128)(2,1)S(1)}, u32[]{:S(2)}, u32[]{:S(2)}) collective-permute-start(bf16[128,768]{1,0:T(8,128)(2,1)} %get-tuple-element.53), channel_id=1, source_target_pairs={{0,1},{1,2},{2,3},{3,4},{4,5},{5,6},{6,7},{7,8},{8,9},{9,10},{10,1... | collective-permute-start | bytes 589832 | tf_op jit(solution)/shard_map/ppermute | solution.py:315
  5.6 6.6 %collective-permute-start.2 = (bf16[128,768]{1,0:T(8,128)(2,1)}, bf16[128,768]{1,0:T(8,128)(2,1)S(1)}, u32[]{:S(2)}, u32[]{:S(2)}) collective-permute-start(bf16[128,768]{1,0:T(8,128)(2,1)} %get-tuple-element.53), channel_id=1, source_target_pairs={{0,31},{1,0},{2,1},{3,2},{4,3},{5,4},{6,5},{7,6},{8,7},{9,8},{10,9... | collective-permute-start | bytes 589832 | tf_op jit(solution)/shard_map/ppermute | solution.py:315
  12.2 2.9 %collective-permute-start.4 = (bf16[32,768]{1,0:T(8,128)(2,1)}, bf16[32,768]{1,0:T(8,128)(2,1)S(1)}, u32[]{:S(2)}, u32[]{:S(2)}) collective-permute-start(bf16[32,768]{1,0:T(8,128)(2,1)} %get-tuple-element.56), channel_id=1, source_target_pairs={{0,128},{32,160},{64,192},{96,224},{128,0},{160,32},{192,64},{224,... | collective-permute-start | bytes 147464 | tf_op jit(solution)/shard_map/ppermute | solution.py:315
  15.1 3.8 %collective-permute-start = (bf16[48,768]{1,0:T(8,128)(2,1)}, bf16[48,768]{1,0:T(8,128)(2,1)S(1)}, u32[]{:S(2)}, u32[]{:S(2)}) collective-permute-start(bf16[48,768]{1,0:T(8,128)(2,1)} %get-tuple-element.68), channel_id=1, source_target_pairs={{0,16},{1,17},{2,18},{3,19},{4,20},{5,21},{6,22},{7,23},{8,24},{9,... | collective-permute-start | bytes 221192 | tf_op jit(solution)/shard_map/ppermute | solution.py:315
  19.4 2.3 %collective-permute-start.5 = (bf16[32,768]{1,0:T(8,128)(2,1)}, bf16[32,768]{1,0:T(8,128)(2,1)S(1)}, u32[]{:S(2)}, u32[]{:S(2)}) collective-permute-start(bf16[32,768]{1,0:T(8,128)(2,1)} %get-tuple-element.57), channel_id=1, source_target_pairs={{0,192},{32,224},{64,0},{96,32},{128,64},{160,96},{192,128},{224,1... | collective-permute-start | bytes 147464 | tf_op jit(solution)/shard_map/ppermute | solution.py:315
  24.9 2.7 %collective-permute-start.7 = (bf16[96,768]{1,0:T(8,128)(2,1)S(1)}, bf16[96,768]{1,0:T(8,128)(2,1)S(1)}, u32[]{:S(2)}, u32[]{:S(2)}) collective-permute-start(bf16[96,768]{1,0:T(8,128)(2,1)S(1)} %get-tuple-element.99), channel_id=1, source_target_pairs={{0,28},{1,29},{2,30},{3,31},{4,0},{5,1},{6,2},{7,3},{8,4},{9,5},{1... | collective-permute-start | bytes 442376 | tf_op jit(solution)/shard_map/ppermute | solution.py:323
  27.6 2.0 %copy-done = bf16[768,2304]{1,0:T(8,128)(2,1)S(1)} copy-done((bf16[768,2304]{1,0:T(8,128)(2,1)S(1)}, bf16[768,2304]{1,0:T(8,128)(2,1)}, u32[]{:S(2)}) %copy-start) | copy-done | bytes 3538968
  31.3 1.8 %collective-permute-done.8 = bf16[96,768]{1,0:T(8,128)(2,1)S(1)} collective-permute-done((bf16[96,768]{1,0:T(8,128)(2,1)S(1)}, bf16[96,768]{1,0:T(8,128)(2,1)S(1)}, u32[]{:S(2)}, u32[]{:S(2)}) %collective-permute-start.8) | collective-permute-done | bytes 147488 | tf_op jit(solution)/shard_map/ppermute | solution.py:323
  33.2 2.7 %collective-permute-start.14 = (bf16[384,768]{1,0:T(8,128)(2,1)S(1)}, bf16[384,768]{1,0:T(8,128)(2,1)S(1)}, u32[]{:S(2)}, u32[]{:S(2)}) collective-permute-start(bf16[384,768]{1,0:T(8,128)(2,1)S(1)} %constant_dynamic-update-slice_fusion.2), channel_id=1, source_target_pairs={{0,3},{1,0},{2,1},{3,2},{4,7},{5,4},{6,5},{7,6},{8,11},{9,8},{10,9... | collective-permute-start | bytes 1769480 | tf_op jit(solution)/shard_map/ppermute | solution.py:323
  35.9 8.1 %collective-permute-start.9 = (bf16[144,1536]{1,0:T(8,128)(2,1)S(1)}, bf16[144,1536]{1,0:T(8,128)(2,1)S(1)}, u32[]{:S(2)}, u32[]{:S(2)}) collective-permute-start(bf16[144,1536]{1,0:T(8,128)(2,1)S(1)} %get-tuple-element.71.refs_1_), channel_id=1, source_target_pairs={{0,32},{32,0},{64,96},{96,64},{128,160},{160,128},{192,224},{224,1... | collective-permute-start | bytes 1327112 | tf_op jit(solution)/shard_map/ppermute | solution.py:315
  44.0 1.5 %shard_map.146 = (bf16[128,768]{1,0:T(8,128)(2,1)S(1)}, bf16[384,1536]{1,0:T(8,128)(2,1)S(1)}) custom-call(s32[1]{0:T(128)S(6)} %copy.28.level, bf16[128,768]{1,0:T(8,128)(2,1)S(1)} %bitcast.5, s32[2,64]{1,0:T(2,128)S(1)} %copy-done.10, f32[768]{0:T(1024)S(1)} %copy-done.8, f32[16,768]{1,0:T(8,128)S(1)} %copy-done.6, ...), custom_call_target="tpu_custom_call" | custom-call | bytes 1 | tf_op jit(solution)/shard_map/pallas_call | solution.py:72
  46.8 4.1 %collective-permute-start.11 = (bf16[32,768]{1,0:T(8,128)(2,1)S(1)}, bf16[32,768]{1,0:T(8,128)(2,1)S(1)}, u32[]{:S(2)}, u32[]{:S(2)}) collective-permute-start(bf16[32,768]{1,0:T(8,128)(2,1)S(1)} %get-tuple-element.74), channel_id=1, source_target_pairs={{0,128},{32,160},{64,192},{96,224},{128,0},{160,32},{192,64},{224,... | collective-permute-start | bytes 147464 | tf_op jit(solution)/shard_map/ppermute | solution.py:315
  54.9 2.3 %collective-permute-done.15 = bf16[384,768]{1,0:T(8,128)(2,1)S(1)} collective-permute-done((bf16[384,768]{1,0:T(8,128)(2,1)S(1)}, bf16[384,768]{1,0:T(8,128)(2,1)S(1)}, u32[]{:S(2)}, u32[]{:S(2)}) %collective-permute-start.15) | collective-permute-done | bytes 589856 | tf_op jit(solution)/shard_map/ppermute | solution.py:323
  58.7 3.4 %shard_map.149.refs_5_ = f32[128,768]{1,0:T(8,128)S(1)} custom-call(s32[1]{0:T(128)S(6)} %copy.28.level, s32[2,6]{1,0:T(2,128)S(1)} %copy-done.11, s32[64]{0:T(128)S(1)} %copy-done.12, bf16[128,768]{1,0:T(8,128)(2,1)S(1)} %get-tuple-element.60.refs_3_.refs_2_, bf16[384,1536]{1,0:T(8,128)(2,1)S(1)} %get-tuple-element.61.refs_3_, ...), custom_call_target="tpu_custom_call" | custom-call | bytes 1 | tf_op jit(solution)/shard_map/pallas_call | solution.py:72
  63.5 3.0 %shard_map.150 = (bf16[128,768]{1,0:T(8,128)(2,1)S(1)}, bf16[128,768]{1,0:T(8,128)(2,1)S(1)}, bf16[32,768]{1,0:T(8,128)(2,1)S(1)}, bf16[32,768]{1,0:T(8,128)(2,1...) custom-call(s32[1]{0:T(128)S(6)} %copy.28.level, f32[16]{0:T(128)S(1)} %copy-done.13, ...), custom_call_target="tpu_custom_call" | custom-call | bytes 1 | tf_op jit(solution)/shard_map/pallas_call | solution.py:72
  66.9 3.3 %collective-permute-start.21 = (bf16[128,768]{1,0:T(8,128)(2,1)S(1)}, bf16[128,768]{1,0:T(8,128)(2,1)S(1)}, u32[]{:S(2)}, u32[]{:S(2)}) collective-permute-start(bf16[128,768]{1,0:T(8,128)(2,1)S(1)} %get-tuple-element.86), channel_id=1, source_target_pairs={{0,225},{1,226},{2,227},{3,228},{4,229},{5,230},{6,231},{7,232},{8... | collective-permute-start | bytes 589832 | tf_op jit(solution)/shard_map/ppermute | solution.py:323
  70.2 4.4 %collective-permute-start.22 = (bf16[128,768]{1,0:T(8,128)(2,1)S(1)}, bf16[128,768]{1,0:T(8,128)(2,1)S(1)}, u32[]{:S(2)}, u32[]{:S(2)}) collective-permute-start(bf16[128,768]{1,0:T(8,128)(2,1)S(1)} %get-tuple-element.86), channel_id=1, source_target_pairs={{0,255},{1,224},{2,225},{3,226},{4,227},{5,228},{6,229},{7,230},{8... | collective-permute-start | bytes 589832 | tf_op jit(solution)/shard_map/ppermute | solution.py:323
  76.0 3.7 %collective-permute-done.24.refs_1_ = bf16[32,768]{1,0:T(8,128)(2,1)S(1)} collective-permute-done((bf16[32,768]{1,0:T(8,128)(2,1)S(1)}, bf16[32,768]{1,0:T(8,128)(2,1)S(1)}, u32[]{:S(2)}, u32[]{:S(2)}) %collective-permute-start.24) | collective-permute-done | bytes 49184 | tf_op jit(solution)/shard_map/ppermute | solution.py:315
  79.7 1.7 %collective-permute-done.25.refs_2_ = bf16[32,768]{1,0:T(8,128)(2,1)S(1)} collective-permute-done((bf16[32,768]{1,0:T(8,128)(2,1)S(1)}, bf16[32,768]{1,0:T(8,128)(2,1)S(1)}, u32[]{:S(2)}, u32[]{:S(2)}) %collective-permute-start.25) | collective-permute-done | bytes 49184 | tf_op jit(solution)/shard_map/ppermute | solution.py:315
  81.4 2.0 %collective-permute-done.26.refs_3_ = bf16[32,768]{1,0:T(8,128)(2,1)S(1)} collective-permute-done((bf16[32,768]{1,0:T(8,128)(2,1)S(1)}, bf16[32,768]{1,0:T(8,128)(2,1)S(1)}, u32[]{:S(2)}, u32[]{:S(2)}) %collective-permute-start.26) | collective-permute-done | bytes 49184 | tf_op jit(solution)/shard_map/ppermute | solution.py:315
  87.4 2.0 %collective-permute-start.29 = (bf16[32,768]{1,0:T(8,128)(2,1)S(1)}, bf16[32,768]{1,0:T(8,128)(2,1)S(1)}, u32[]{:S(2)}, u32[]{:S(2)}) collective-permute-start(bf16[32,768]{1,0:T(8,128)(2,1)S(1)} %get-tuple-element.97), channel_id=1, source_target_pairs={{0,128},{32,160},{64,192},{96,224},{128,0},{160,32},{192,64},{224,... | collective-permute-start | bytes 147464 | tf_op jit(solution)/shard_map/ppermute | solution.py:315
  90.1 3.4 %shard_map.152.refs_5_ = f32[128,768]{1,0:T(8,128)S(1)} custom-call(s32[1]{0:T(128)S(6)} %copy.28.level, s32[2,6]{1,0:T(2,128)S(1)} %copy-done.11, s32[64]{0:T(128)S(1)} %copy-done.12, bf16[128,768]{1,0:T(8,128)(2,1)S(1)} %get-tuple-element.87.refs_2_.refs_3_, bf16[384,1536]{1,0:T(8,128)(2,1)S(1)} %get-tuple-element.88.refs_3_, bf16[768,768]{1,0:T(8,128)(2,1)S(1)} %copy-done.3), custom_call_target="tpu_custom_call" | custom-call | bytes 1 | tf_op jit(solution)/shard_map/pallas_call | solution.py:72
  93.6 3.5 %shard_map.155 = bf16[128,768]{1,0:T(8,128)(2,1)} custom-call(s32[1]{0:T(128)S(6)} %copy.28.level, f32[16]{0:T(128)S(1)} %copy-done.13, bf16[128,768]{1,0:T(8,128)(2,1)S(1)} %collective-permute-done.20.refs_0_.refs_5_.refs_1_, s32[2,64]{1,0:T(2,128)S(1)} %copy-done.10, f32[768]{0:T(1024)S(1)} %copy-done.8, f32[16,768]{1,0:T(8,128)S(1)} %copy-done.6, ...), custom_call_target="tpu_custom_call" | custom-call | bytes 1 | tf_op jit(solution)/shard_map/pallas_call | solution.py:72
  (90 shorter events, 19.9 us)
Async XLA Ops:
  3.5 20.4 %collective-permute-start.1 = (bf16[128,768]{1,0:T(8,128)(2,1)}, bf16[128,768]{1,0:T(8,128)(2,1)S(1)}, u32[]{:S(2)}, u32[]{:S(2)}) collective-permute-start(bf16[128,768]{1,0:T(8,128)(2,1)} %get-tuple-element.53), channel_id=1, source_target_pairs={{0,1},{1,2},{2,3},{3,4},{4,5},{5,6},{6,7},{7,8},{8,9},{9,10},{10,1... | collective-permute-start | bytes 589832 | tf_op jit(solution)/shard_map/ppermute | solution.py:315
  5.6 18.3 %collective-permute-start.2 = (bf16[128,768]{1,0:T(8,128)(2,1)}, bf16[128,768]{1,0:T(8,128)(2,1)S(1)}, u32[]{:S(2)}, u32[]{:S(2)}) collective-permute-start(bf16[128,768]{1,0:T(8,128)(2,1)} %get-tuple-element.53), channel_id=1, source_target_pairs={{0,31},{1,0},{2,1},{3,2},{4,3},{5,4},{6,5},{7,6},{8,7},{9,8},{10,9... | collective-permute-start | bytes 589832 | tf_op jit(solution)/shard_map/ppermute | solution.py:315
  12.2 7.2 %collective-permute-start.4 = (bf16[32,768]{1,0:T(8,128)(2,1)}, bf16[32,768]{1,0:T(8,128)(2,1)S(1)}, u32[]{:S(2)}, u32[]{:S(2)}) collective-permute-start(bf16[32,768]{1,0:T(8,128)(2,1)} %get-tuple-element.56), channel_id=1, source_target_pairs={{0,128},{32,160},{64,192},{96,224},{128,0},{160,32},{192,64},{224,... | collective-permute-start | bytes 147464 | tf_op jit(solution)/shard_map/ppermute | solution.py:315
  15.1 8.0 %collective-permute-start = (bf16[48,768]{1,0:T(8,128)(2,1)}, bf16[48,768]{1,0:T(8,128)(2,1)S(1)}, u32[]{:S(2)}, u32[]{:S(2)}) collective-permute-start(bf16[48,768]{1,0:T(8,128)(2,1)} %get-tuple-element.68), channel_id=1, source_target_pairs={{0,16},{1,17},{2,18},{3,19},{4,20},{5,21},{6,22},{7,23},{8,24},{9,... | collective-permute-start | bytes 221192 | tf_op jit(solution)/shard_map/ppermute | solution.py:315
  19.0 4.9 %collective-permute-start.3 = (bf16[48,768]{1,0:T(8,128)(2,1)}, bf16[48,768]{1,0:T(8,128)(2,1)S(1)}, u32[]{:S(2)}, u32[]{:S(2)}) collective-permute-start(bf16[48,768]{1,0:T(8,128)(2,1)} %get-tuple-element.55), channel_id=1, source_target_pairs={{0,64},{32,96},{64,128},{96,160},{128,192},{160,224},{192,0},{224,... | collective-permute-start | bytes 221192 | tf_op jit(solution)/shard_map/ppermute | solution.py:315
  24.8 6.2 %collective-permute-start.6 = (bf16[96,768]{1,0:T(8,128)(2,1)S(1)}, bf16[96,768]{1,0:T(8,128)(2,1)S(1)}, u32[]{:S(2)}, u32[]{:S(2)}) collective-permute-start(bf16[96,768]{1,0:T(8,128)(2,1)S(1)} %get-tuple-element.99), channel_id=1, source_target_pairs={{0,4},{1,5},{2,6},{3,7},{4,8},{5,9},{6,10},{7,11},{8,12},{9,13},{1... | collective-permute-start | bytes 442376 | tf_op jit(solution)/shard_map/ppermute | solution.py:323
  24.9 6.3 %collective-permute-start.7 = (bf16[96,768]{1,0:T(8,128)(2,1)S(1)}, bf16[96,768]{1,0:T(8,128)(2,1)S(1)}, u32[]{:S(2)}, u32[]{:S(2)}) collective-permute-start(bf16[96,768]{1,0:T(8,128)(2,1)S(1)} %get-tuple-element.99), channel_id=1, source_target_pairs={{0,28},{1,29},{2,30},{3,31},{4,0},{5,1},{6,2},{7,3},{8,4},{9,5},{1... | collective-permute-start | bytes 442376 | tf_op jit(solution)/shard_map/ppermute | solution.py:323
  27.6 5.5 %collective-permute-start.8 = (bf16[96,768]{1,0:T(8,128)(2,1)S(1)}, bf16[96,768]{1,0:T(8,128)(2,1)S(1)}, u32[]{:S(2)}, u32[]{:S(2)}) collective-permute-start(bf16[96,768]{1,0:T(8,128)(2,1)S(1)} %get-tuple-element.99), channel_id=1, source_target_pairs={{0,8},{1,9},{2,10},{3,11},{4,12},{5,13},{6,14},{7,15},{8,16},{9,17... | collective-permute-start | bytes 442376 | tf_op jit(solution)/shard_map/ppermute | solution.py:323
  33.1 21.8 %collective-permute-start.13 = (bf16[384,768]{1,0:T(8,128)(2,1)S(1)}, bf16[384,768]{1,0:T(8,128)(2,1)S(1)}, u32[]{:S(2)}, u32[]{:S(2)}) collective-permute-start(bf16[384,768]{1,0:T(8,128)(2,1)S(1)} %constant_dynamic-update-slice_fusion.2), channel_id=1, source_target_pairs={{0,1},{1,2},{2,3},{3,0},{4,5},{5,6},{6,7},{7,4},{8,9},{9,10},{10,1... | collective-permute-start | bytes 1769480 | tf_op jit(solution)/shard_map/ppermute | solution.py:323
  33.2 21.7 %collective-permute-start.14 = (bf16[384,768]{1,0:T(8,128)(2,1)S(1)}, bf16[384,768]{1,0:T(8,128)(2,1)S(1)}, u32[]{:S(2)}, u32[]{:S(2)}) collective-permute-start(bf16[384,768]{1,0:T(8,128)(2,1)S(1)} %constant_dynamic-update-slice_fusion.2), channel_id=1, source_target_pairs={{0,3},{1,0},{2,1},{3,2},{4,7},{5,4},{6,5},{7,6},{8,11},{9,8},{10,9... | collective-permute-start | bytes 1769480 | tf_op jit(solution)/shard_map/ppermute | solution.py:323
  35.9 21.3 %collective-permute-start.15 = (bf16[384,768]{1,0:T(8,128)(2,1)S(1)}, bf16[384,768]{1,0:T(8,128)(2,1)S(1)}, u32[]{:S(2)}, u32[]{:S(2)}) collective-permute-start(bf16[384,768]{1,0:T(8,128)(2,1)S(1)} %constant_dynamic-update-slice_fusion.2), channel_id=1, source_target_pairs={{0,2},{1,3},{2,0},{3,1},{4,6},{5,7},{6,4},{7,5},{8,10},{9,11},{10,... | collective-permute-start | bytes 1769480 | tf_op jit(solution)/shard_map/ppermute | solution.py:323
  35.9 9.6 %collective-permute-start.9 = (bf16[144,1536]{1,0:T(8,128)(2,1)S(1)}, bf16[144,1536]{1,0:T(8,128)(2,1)S(1)}, u32[]{:S(2)}, u32[]{:S(2)}) collective-permute-start(bf16[144,1536]{1,0:T(8,128)(2,1)S(1)} %get-tuple-element.71.refs_1_), channel_id=1, source_target_pairs={{0,32},{32,0},{64,96},{96,64},{128,160},{160,128},{192,224},{224,1... | collective-permute-start | bytes 1327112 | tf_op jit(solution)/shard_map/ppermute | solution.py:315
  46.7 5.0 %collective-permute-start.10 = (bf16[32,768]{1,0:T(8,128)(2,1)S(1)}, bf16[32,768]{1,0:T(8,128)(2,1)S(1)}, u32[]{:S(2)}, u32[]{:S(2)}) collective-permute-start(bf16[32,768]{1,0:T(8,128)(2,1)S(1)} %get-tuple-element.73), channel_id=1, source_target_pairs={{0,64},{32,96},{64,128},{96,160},{128,192},{160,224},{192,0},{224,... | collective-permute-start | bytes 147464 | tf_op jit(solution)/shard_map/ppermute | solution.py:315
  46.8 6.8 %collective-permute-start.11 = (bf16[32,768]{1,0:T(8,128)(2,1)S(1)}, bf16[32,768]{1,0:T(8,128)(2,1)S(1)}, u32[]{:S(2)}, u32[]{:S(2)}) collective-permute-start(bf16[32,768]{1,0:T(8,128)(2,1)S(1)} %get-tuple-element.74), channel_id=1, source_target_pairs={{0,128},{32,160},{64,192},{96,224},{128,0},{160,32},{192,64},{224,... | collective-permute-start | bytes 147464 | tf_op jit(solution)/shard_map/ppermute | solution.py:315
  57.2 5.2 %collective-permute-start.16 = (bf16[384,768]{1,0:T(8,128)(2,1)S(1)}, bf16[384,768]{1,0:T(8,128)(2,1)S(1)}, u32[]{:S(2)}, u32[]{:S(2)}) collective-permute-start(bf16[384,768]{1,0:T(8,128)(2,1)S(1)} %constant_dynamic-update-slice_fusion.2), channel_id=1, source_target_pairs={{0,32},{32,0},{64,96},{96,64},{128,160},{160,128},{192,224},{224,1... | collective-permute-start | bytes 1769480 | tf_op jit(solution)/shard_map/ppermute | solution.py:315
  58.1 4.3 %collective-permute-start.17 = (bf16[384,768]{1,0:T(8,128)(2,1)S(1)}, bf16[384,768]{1,0:T(8,128)(2,1)S(1)}, u32[]{:S(2)}, u32[]{:S(2)}) collective-permute-start(bf16[384,768]{1,0:T(8,128)(2,1)S(1)} %collective-permute-done.13), channel_id=1, source_target_pairs={{0,32},{32,0},{64,96},{96,64},{128,160},{160,128},{192,224},{224,1... | collective-permute-start | bytes 1769480 | tf_op jit(solution)/shard_map/ppermute | solution.py:315
  58.2 4.3 %collective-permute-start.18 = (bf16[384,768]{1,0:T(8,128)(2,1)S(1)}, bf16[384,768]{1,0:T(8,128)(2,1)S(1)}, u32[]{:S(2)}, u32[]{:S(2)}) collective-permute-start(bf16[384,768]{1,0:T(8,128)(2,1)S(1)} %collective-permute-done.14), channel_id=1, source_target_pairs={{0,32},{32,0},{64,96},{96,64},{128,160},{160,128},{192,224},{224,1... | collective-permute-start | bytes 1769480 | tf_op jit(solution)/shard_map/ppermute | solution.py:315
  66.4 17.0 %collective-permute-start.20 = (bf16[128,768]{1,0:T(8,128)(2,1)S(1)}, bf16[128,768]{1,0:T(8,128)(2,1)S(1)}, u32[]{:S(2)}, u32[]{:S(2)}) collective-permute-start(bf16[128,768]{1,0:T(8,128)(2,1)S(1)} %get-tuple-element.85), channel_id=1, source_target_pairs={{0,224},{32,0},{64,32},{96,64},{128,96},{160,128},{192,160},{224,1... | collective-permute-start | bytes 589832 | tf_op jit(solution)/shard_map/ppermute | solution.py:315
  66.9 16.6 %collective-permute-start.21 = (bf16[128,768]{1,0:T(8,128)(2,1)S(1)}, bf16[128,768]{1,0:T(8,128)(2,1)S(1)}, u32[]{:S(2)}, u32[]{:S(2)}) collective-permute-start(bf16[128,768]{1,0:T(8,128)(2,1)S(1)} %get-tuple-element.86), channel_id=1, source_target_pairs={{0,225},{1,226},{2,227},{3,228},{4,229},{5,230},{6,231},{7,232},{8... | collective-permute-start | bytes 589832 | tf_op jit(solution)/shard_map/ppermute | solution.py:323
  70.2 13.3 %collective-permute-start.22 = (bf16[128,768]{1,0:T(8,128)(2,1)S(1)}, bf16[128,768]{1,0:T(8,128)(2,1)S(1)}, u32[]{:S(2)}, u32[]{:S(2)}) collective-permute-start(bf16[128,768]{1,0:T(8,128)(2,1)S(1)} %get-tuple-element.86), channel_id=1, source_target_pairs={{0,255},{1,224},{2,225},{3,226},{4,227},{5,228},{6,229},{7,230},{8... | collective-permute-start | bytes 589832 | tf_op jit(solution)/shard_map/ppermute | solution.py:323
  74.7 5.0 %collective-permute-start.24 = (bf16[32,768]{1,0:T(8,128)(2,1)S(1)}, bf16[32,768]{1,0:T(8,128)(2,1)S(1)}, u32[]{:S(2)}, u32[]{:S(2)}) collective-permute-start(bf16[32,768]{1,0:T(8,128)(2,1)S(1)} %get-tuple-element.90), channel_id=1, source_target_pairs={{0,96},{32,64},{64,160},{96,128},{128,224},{160,192},{192,32},{224... | collective-permute-start | bytes 147464 | tf_op jit(solution)/shard_map/ppermute | solution.py:315
  75.9 5.5 %collective-permute-start.25 = (bf16[32,768]{1,0:T(8,128)(2,1)S(1)}, bf16[32,768]{1,0:T(8,128)(2,1)S(1)}, u32[]{:S(2)}, u32[]{:S(2)}) collective-permute-start(bf16[32,768]{1,0:T(8,128)(2,1)S(1)} %get-tuple-element.91), channel_id=1, source_target_pairs={{0,160},{32,128},{64,224},{96,192},{128,32},{160,0},{192,96},{224,... | collective-permute-start | bytes 147464 | tf_op jit(solution)/shard_map/ppermute | solution.py:315
  87.3 6.2 %collective-permute-start.28 = (bf16[32,768]{1,0:T(8,128)(2,1)S(1)}, bf16[32,768]{1,0:T(8,128)(2,1)S(1)}, u32[]{:S(2)}, u32[]{:S(2)}) collective-permute-start(bf16[32,768]{1,0:T(8,128)(2,1)S(1)} %get-tuple-element.96), channel_id=1, source_target_pairs={{0,64},{32,96},{64,128},{96,160},{128,192},{160,224},{192,0},{224,... | collective-permute-start | bytes 147464 | tf_op jit(solution)/shard_map/ppermute | solution.py:315
  87.4 6.1 %collective-permute-start.29 = (bf16[32,768]{1,0:T(8,128)(2,1)S(1)}, bf16[32,768]{1,0:T(8,128)(2,1)S(1)}, u32[]{:S(2)}, u32[]{:S(2)}) collective-permute-start(bf16[32,768]{1,0:T(8,128)(2,1)S(1)} %get-tuple-element.97), channel_id=1, source_target_pairs={{0,128},{32,160},{64,192},{96,224},{128,0},{160,32},{192,64},{224,... | collective-permute-start | bytes 147464 | tf_op jit(solution)/shard_map/ppermute | solution.py:315
  (21 other events, 335.3 us)
